TPU v7x, 128 devices: a whole 4x4x4 slice. The times are simulated.
128 devices in a mesh: ctx: 32 (over z_lo, x, y), tp: 4 (over z_hi, core).
Axes of the slice: x: 4, y: 4, z: 4 (z_hi: 2, z_lo: 2; z = z_hi * 2 + z_lo), core: 2. Of those that a mesh axis runs over, the one named last changes fastest.
Arguments:
- new_queries: bfloat16 [2048, 8192], P('ctx', 'tp'), may hold values from -24 to 24
- new_keys: bfloat16 [2048, 512], P('ctx', 'tp'), may hold values from -6 to 6
- new_values: bfloat16 [2048, 512], P('ctx', 'tp'), may hold values from -6 to 6
- cache_keys: bfloat16 [32768, 512], P('ctx', 'tp'), may hold values from -24 to 24
- cache_values: bfloat16 [32768, 512], P('ctx', 'tp'), may hold values from -6 to 6
- out_weight: bfloat16 [8192, 16384], P('tp', 'ctx'), may hold values from -0.0625 to 0.0625
- cache_docs: int32 [256], replicated, may hold values from 0 to 3
- new_docs: int32 [16], replicated, may hold values from 0 to 3
- slot_tile: int32 [32], replicated, may hold values from 0 to 31, each once
Outputs:
- projected: bfloat16 [2048, 16384], P('tp', 'ctx')
Inputs may be any that keep to these rules, and one draw needn't show every extreme that they name: `slot_tile`: each number once.
All inputs are finite; a program needn't handle non-finite values.
Results may differ from a plain program's by a relative error of at most 0.02.
Values may be sent and summed in bfloat16 or wider, within the bound.
A program may use at most 64 MiB of HBM per device.

v0:
```python
import jax
import jax.numpy as jnp
from jax import lax
from jax.sharding import PartitionSpec as P

HD = 128
BLK = 128


NEGATIVE = -1e30


def from_behind(block, axis, distance):
    devices = range(lax.axis_size(axis))
    route = [((i - distance) % len(devices), i) for i in devices]
    return lax.ppermute(block, axis, route)


def query_info(slot_tile, new_docs, source, query_rows):
    position = slot_tile[source] * query_rows + jnp.arange(query_rows, dtype=jnp.int32)
    return (position, new_docs[position // BLK])


def key_info(cache_docs, slot_tile, new_docs, source, cache_rows, query_rows):
    cache_index = source * cache_rows + jnp.arange(cache_rows, dtype=jnp.int32)
    new_position, new_doc = query_info(slot_tile, new_docs, source, query_rows)
    position = jnp.concatenate([jnp.full((cache_rows,), -1, jnp.int32), new_position])
    return (position, jnp.concatenate([cache_docs[cache_index // BLK], new_doc]))


def partial_tile(queries, stacked, query_position, query_doc, key_position, key_doc):
    query_rows = queries.shape[0]
    kv_count = stacked.shape[2] // HD
    group_size = queries.shape[1] // (kv_count * HD)
    grouped = queries.reshape(query_rows, kv_count, group_size, HD)
    key_rows = stacked[0].reshape(-1, kv_count, HD)
    value_rows = stacked[1].reshape(-1, kv_count, HD)
    scores = jnp.einsum(
        "rgjd,kgd->gjrk", grouped, key_rows, preferred_element_type=jnp.float32
    ) * HD ** (-0.5)
    allowed = (query_doc[:, None] == key_doc[None, :]) & (
        key_position[None, :] <= query_position[:, None]
    )
    scores = jnp.where(allowed[None, None], scores, NEGATIVE)
    maxima = jnp.max(scores, axis=3)
    weights = jnp.exp(scores - maxima[..., None])
    totals = jnp.sum(weights, axis=3)
    mixture = jnp.einsum(
        "gjrk,kgd->rgjd",
        weights.astype(jnp.bfloat16),
        value_rows,
        preferred_element_type=jnp.float32,
    )
    maxima_rows = jnp.transpose(maxima, (2, 0, 1))
    totals_rows = jnp.transpose(totals, (2, 0, 1))
    partial_value = (mixture / totals_rows[..., None]).astype(jnp.bfloat16).reshape(query_rows, -1)
    return (partial_value, maxima_rows.reshape(query_rows, -1), totals_rows.reshape(query_rows, -1))


def merge_home(pieces):
    outputs, maxima, totals = pieces
    count, query_rows, features = outputs.shape
    head_count = maxima.shape[2]
    largest = jnp.max(maxima, axis=0)
    scaling = jnp.exp(maxima - largest[None]) * totals
    normalizer = jnp.sum(scaling, axis=0)
    weighted = jnp.einsum(
        "crh,crhd->rhd",
        scaling,
        outputs.reshape(count, query_rows, head_count, -1).astype(jnp.float32),
    )
    return (weighted / normalizer[..., None]).astype(jnp.bfloat16).reshape(query_rows, features)


def travel(moving_tile, running, visit, members, myself):
    running = visit(moving_tile, myself, 1.0, running)

    def turn(turn_index, carried):
        current, inner_state = carried
        current = from_behind(current, "ctx", 1)
        return (current, visit(current, (myself - turn_index) % members, 1.0, inner_state))

    return lax.fori_loop(1, members, turn, (moving_tile, running))[1]


def shards(
    new_queries,
    new_keys,
    new_values,
    cache_keys,
    cache_values,
    out_weight,
    cache_docs,
    new_docs,
    slot_tile,
):
    members = lax.axis_size("ctx")
    myself = lax.axis_index("ctx")
    query_rows = new_queries.shape[0]
    cache_rows = cache_keys.shape[0]
    features = new_queries.shape[1]
    head_count = features // HD
    own_stacked = jnp.stack(
        [jnp.concatenate([cache_keys, new_keys], 0), jnp.concatenate([cache_values, new_values], 0)]
    )
    own_key_position, own_key_doc = key_info(
        cache_docs, slot_tile, new_docs, myself, cache_rows, query_rows
    )

    def visit(moving_tile, source, counted, running):
        outputs, maxima_all, totals_all = running
        query_position, query_doc = query_info(slot_tile, new_docs, source, query_rows)
        partial_value, maxima, totals = partial_tile(
            moving_tile, own_stacked, query_position, query_doc, own_key_position, own_key_doc
        )
        outputs = lax.dynamic_update_index_in_dim(outputs, partial_value, source, 0)
        maxima_all = lax.dynamic_update_index_in_dim(maxima_all, maxima, source, 0)
        totals_all = lax.dynamic_update_index_in_dim(totals_all, totals, source, 0)
        return (outputs, maxima_all, totals_all)

    start = (
        jnp.zeros((members, query_rows, features), jnp.bfloat16),
        jnp.zeros((members, query_rows, head_count), jnp.float32),
        jnp.ones((members, query_rows, head_count), jnp.float32),
    )
    outputs, maxima_all, totals_all = travel(new_queries, start, visit, members, myself)
    attended = merge_home(
        (
            lax.all_to_all(
                outputs.astype(jnp.float32), "ctx", split_axis=0, concat_axis=0, tiled=True
            ).astype(outputs.dtype),
            lax.all_to_all(maxima_all, "ctx", split_axis=0, concat_axis=0, tiled=True),
            lax.all_to_all(totals_all, "ctx", split_axis=0, concat_axis=0, tiled=True),
        )
    )
    head_terms = jnp.dot(
        lax.all_gather(attended, "ctx", axis=0, tiled=True),
        out_weight,
        preferred_element_type=jnp.float32,
    )
    return lax.psum_scatter(head_terms.astype(jnp.bfloat16), "tp", scatter_dimension=0, tiled=True)


def solution(mesh):
    return jax.shard_map(
        shards,
        mesh=mesh,
        in_specs=(
            P("ctx", "tp"),
            P("ctx", "tp"),
            P("ctx", "tp"),
            P("ctx", "tp"),
            P("ctx", "tp"),
            P("tp", "ctx"),
            P(),
            P(),
            P(),
        ),
        out_specs=P("tp", "ctx"),
        check_vma=False,
    )
```

profile of v0, /device:TPU:1, one launch (start us, length us, event | category | flops | bytes accessed | tf_op | source)
XLA Modules:
  0.0 931.0 jit_solution(1824851861747515106)
XLA Ops:
  27.2 499.1 %while.21 = (s32[]{:T(128)}, bf16[64,2048]{1,0:T(8,128)(2,1)S(1)}, bf16[32,64,2048]{2,1,0:T(8,128)(2,1)}, f32[32,64,16]{1,2,0:T(8,128)}, f32[32,64,16]{1,2,0:T(8...) while((s32[]{:T(128)}, bf16[64,2048]{1,0:T(8,128)(2,1)S(1)}, ...), condition=%wide.region_5.6_spmd, body=%wide.region_2.5_spmd.sunk | while | flops 580923648 | bytes 17935240 | solution.py:83
  31.5 8.9 collective-permute-done
  48.6 8.6 collective-permute-done
  65.4 7.7 collective-permute-done
  81.3 7.3 collective-permute-done
  174.2 7.3 collective-permute-done
  220.6 7.4 collective-permute-done
  236.2 8.4 collective-permute-done
  252.8 9.5 %collective-permute-done = bf16[64,2048]{1,0:T(8,128)(2,1)S(1)} collective-permute-done((bf16[64,2048]{1,0:T(8,128)(2,1)S(1)}, bf16[64,2048]{1,0:T(8,128)(2,1)S(1)}, u32[]{:S(2)}, u32[]{:S(2)}) %collective-permute-start) | collective-permute-done | bytes 262176 | tf_op jit(solution)/shard_map/while/body/eval_jaxpr/ppermute | solution.py:16
  270.5 9.8 %collective-permute-done = bf16[64,2048]{1,0:T(8,128)(2,1)S(1)} collective-permute-done((bf16[64,2048]{1,0:T(8,128)(2,1)S(1)}, bf16[64,2048]{1,0:T(8,128)(2,1)S(1)}, u32[]{:S(2)}, u32[]{:S(2)}) %collective-permute-start) | collective-permute-done | bytes 262176 | tf_op jit(solution)/shard_map/while/body/eval_jaxpr/ppermute | solution.py:16
  288.4 8.8 collective-permute-done
  305.5 7.9 collective-permute-done
  352.6 7.3 collective-permute-done
  445.4 7.3 collective-permute-done
  476.4 8.3 collective-permute-done
  492.9 9.3 %collective-permute-done = bf16[64,2048]{1,0:T(8,128)(2,1)S(1)} collective-permute-done((bf16[64,2048]{1,0:T(8,128)(2,1)S(1)}, bf16[64,2048]{1,0:T(8,128)(2,1)S(1)}, u32[]{:S(2)}, u32[]{:S(2)}) %collective-permute-start) | collective-permute-done | bytes 262176 | tf_op jit(solution)/shard_map/while/body/eval_jaxpr/ppermute | solution.py:16
  510.4 10.0 %collective-permute-done = bf16[64,2048]{1,0:T(8,128)(2,1)S(1)} collective-permute-done((bf16[64,2048]{1,0:T(8,128)(2,1)S(1)}, bf16[64,2048]{1,0:T(8,128)(2,1)S(1)}, u32[]{:S(2)}, u32[]{:S(2)}) %collective-permute-start) | collective-permute-done | bytes 262176 | tf_op jit(solution)/shard_map/while/body/eval_jaxpr/ppermute | solution.py:16
  539.4 10.7 %all_to_all.15 = f32[32,1,1024]{2,1,0:T(1,128)S(1)} all-to-all(f32[32,1,1024]{2,1,0:T(1,128)S(1)} %reshape.460), channel_id=1, replica_groups=mesh['ctx'=32,'tp'=4] {'ctx'}, dimensions={0} | all-to-all | bytes 262144 | tf_op jit(solution)/shard_map/all_to_all | solution.py:133
  558.8 57.3 %all-to-all-done.2 = bf16[32,64,2048]{2,1,0:T(8,128)(2,1)} async-done(((bf16[32,64,2048]{2,1,0:T(8,128)(2,1)}), bf16[32,64,2048]{2,1,0:T(8,128)(2,1)}, u32[]{:S(2)}, u32[]{:S(2)}) %all-to-all-start.2) | async-done | bytes 8388640 | tf_op jit(solution)/shard_map/all_to_all | solution.py:129
  616.0 9.8 %copy.25 = bf16[256,8,16,128]{3,2,1,0:T(8,128)(2,1)} copy(bf16[256,8,16,128]{3,1,2,0:T(8,128)(2,1)} %bitcast.61) | data formatting | bytes 16777216
  625.8 8.5 fusion.24
  635.3 221.2 %all-gather.2.cloned.1.call-done = bf16[2048,2048]{1,0:T(8,128)(2,1)} async-done(((bf16[64,2048]{1,0:T(8,128)(2,1)}), bf16[2048,2048]{1,0:T(8,128)(2,1)}) %all-gather.2.cloned.1.call-update) | async-done | bytes 8388624 | tf_op jit(solution)/shard_map/all_gather | solution.py:137
  856.5 9.2 convolution_convert_fusion
  865.7 58.5 %reduce-scatter.2.cloned.1.call-done = bf16[512,512]{1,0:T(8,128)(2,1)} async-done(((bf16[2048,512]{1,0:T(8,128)(2,1)}), bf16[512,512]{1,0:T(8,128)(2,1)}) %reduce-scatter.2.cloned.1.call-update) | async-done | bytes 524304 | tf_op jit(solution)/shard_map/reduce_scatter | solution.py:141
  (544 shorter events, 387.0 us)
Async XLA Ops:
  27.2 13.2 %collective-permute-start = (bf16[64,2048]{1,0:T(8,128)(2,1)S(1)}, bf16[64,2048]{1,0:T(8,128)(2,1)S(1)}, u32[]{:S(2)}, u32[]{:S(2)}) collective-permute-start(bf16[64,2048]{1,0:T(8,128)(2,1)S(1)} %get-tuple-element.430), channel_id=1, source_target_pairs={{124,0},{0,4},{4,8},{8,12},{12,16},{16,20},{20,24},{24,28},{28,32}... | collective-permute-start | bytes 786440 | tf_op jit(solution)/shard_map/while/body/eval_jaxpr/ppermute | solution.py:16
  46.3 10.9 %collective-permute-start = (bf16[64,2048]{1,0:T(8,128)(2,1)S(1)}, bf16[64,2048]{1,0:T(8,128)(2,1)S(1)}, u32[]{:S(2)}, u32[]{:S(2)}) collective-permute-start(bf16[64,2048]{1,0:T(8,128)(2,1)S(1)} %get-tuple-element.430), channel_id=1, source_target_pairs={{124,0},{0,4},{4,8},{8,12},{12,16},{16,20},{20,24},{24,28},{28,32}... | collective-permute-start | bytes 786440 | tf_op jit(solution)/shard_map/while/body/eval_jaxpr/ppermute | solution.py:16
  63.2 9.9 %collective-permute-start = (bf16[64,2048]{1,0:T(8,128)(2,1)S(1)}, bf16[64,2048]{1,0:T(8,128)(2,1)S(1)}, u32[]{:S(2)}, u32[]{:S(2)}) collective-permute-start(bf16[64,2048]{1,0:T(8,128)(2,1)S(1)} %get-tuple-element.430), channel_id=1, source_target_pairs={{124,0},{0,4},{4,8},{8,12},{12,16},{16,20},{20,24},{24,28},{28,32}... | collective-permute-start | bytes 786440 | tf_op jit(solution)/shard_map/while/body/eval_jaxpr/ppermute | solution.py:16
  79.0 9.5 %collective-permute-start = (bf16[64,2048]{1,0:T(8,128)(2,1)S(1)}, bf16[64,2048]{1,0:T(8,128)(2,1)S(1)}, u32[]{:S(2)}, u32[]{:S(2)}) collective-permute-start(bf16[64,2048]{1,0:T(8,128)(2,1)S(1)} %get-tuple-element.430), channel_id=1, source_target_pairs={{124,0},{0,4},{4,8},{8,12},{12,16},{16,20},{20,24},{24,28},{28,32}... | collective-permute-start | bytes 786440 | tf_op jit(solution)/shard_map/while/body/eval_jaxpr/ppermute | solution.py:16
  94.5 9.5 %collective-permute-start = (bf16[64,2048]{1,0:T(8,128)(2,1)S(1)}, bf16[64,2048]{1,0:T(8,128)(2,1)S(1)}, u32[]{:S(2)}, u32[]{:S(2)}) collective-permute-start(bf16[64,2048]{1,0:T(8,128)(2,1)S(1)} %get-tuple-element.430), channel_id=1, source_target_pairs={{124,0},{0,4},{4,8},{8,12},{12,16},{16,20},{20,24},{24,28},{28,32}... | collective-permute-start | bytes 786440 | tf_op jit(solution)/shard_map/while/body/eval_jaxpr/ppermute | solution.py:16
  110.0 9.5 %collective-permute-start = (bf16[64,2048]{1,0:T(8,128)(2,1)S(1)}, bf16[64,2048]{1,0:T(8,128)(2,1)S(1)}, u32[]{:S(2)}, u32[]{:S(2)}) collective-permute-start(bf16[64,2048]{1,0:T(8,128)(2,1)S(1)} %get-tuple-element.430), channel_id=1, source_target_pairs={{124,0},{0,4},{4,8},{8,12},{12,16},{16,20},{20,24},{24,28},{28,32}... | collective-permute-start | bytes 786440 | tf_op jit(solution)/shard_map/while/body/eval_jaxpr/ppermute | solution.py:16
  125.5 9.5 %collective-permute-start = (bf16[64,2048]{1,0:T(8,128)(2,1)S(1)}, bf16[64,2048]{1,0:T(8,128)(2,1)S(1)}, u32[]{:S(2)}, u32[]{:S(2)}) collective-permute-start(bf16[64,2048]{1,0:T(8,128)(2,1)S(1)} %get-tuple-element.430), channel_id=1, source_target_pairs={{124,0},{0,4},{4,8},{8,12},{12,16},{16,20},{20,24},{24,28},{28,32}... | collective-permute-start | bytes 786440 | tf_op jit(solution)/shard_map/while/body/eval_jaxpr/ppermute | solution.py:16
  141.0 9.5 %collective-permute-start = (bf16[64,2048]{1,0:T(8,128)(2,1)S(1)}, bf16[64,2048]{1,0:T(8,128)(2,1)S(1)}, u32[]{:S(2)}, u32[]{:S(2)}) collective-permute-start(bf16[64,2048]{1,0:T(8,128)(2,1)S(1)} %get-tuple-element.430), channel_id=1, source_target_pairs={{124,0},{0,4},{4,8},{8,12},{12,16},{16,20},{20,24},{24,28},{28,32}... | collective-permute-start | bytes 786440 | tf_op jit(solution)/shard_map/while/body/eval_jaxpr/ppermute | solution.py:16
  171.9 9.5 %collective-permute-start = (bf16[64,2048]{1,0:T(8,128)(2,1)S(1)}, bf16[64,2048]{1,0:T(8,128)(2,1)S(1)}, u32[]{:S(2)}, u32[]{:S(2)}) collective-permute-start(bf16[64,2048]{1,0:T(8,128)(2,1)S(1)} %get-tuple-element.430), channel_id=1, source_target_pairs={{124,0},{0,4},{4,8},{8,12},{12,16},{16,20},{20,24},{24,28},{28,32}... | collective-permute-start | bytes 786440 | tf_op jit(solution)/shard_map/while/body/eval_jaxpr/ppermute | solution.py:16
  218.4 9.6 %collective-permute-start = (bf16[64,2048]{1,0:T(8,128)(2,1)S(1)}, bf16[64,2048]{1,0:T(8,128)(2,1)S(1)}, u32[]{:S(2)}, u32[]{:S(2)}) collective-permute-start(bf16[64,2048]{1,0:T(8,128)(2,1)S(1)} %get-tuple-element.430), channel_id=1, source_target_pairs={{124,0},{0,4},{4,8},{8,12},{12,16},{16,20},{20,24},{24,28},{28,32}... | collective-permute-start | bytes 786440 | tf_op jit(solution)/shard_map/while/body/eval_jaxpr/ppermute | solution.py:16
  233.9 10.7 %collective-permute-start = (bf16[64,2048]{1,0:T(8,128)(2,1)S(1)}, bf16[64,2048]{1,0:T(8,128)(2,1)S(1)}, u32[]{:S(2)}, u32[]{:S(2)}) collective-permute-start(bf16[64,2048]{1,0:T(8,128)(2,1)S(1)} %get-tuple-element.430), channel_id=1, source_target_pairs={{124,0},{0,4},{4,8},{8,12},{12,16},{16,20},{20,24},{24,28},{28,32}... | collective-permute-start | bytes 786440 | tf_op jit(solution)/shard_map/while/body/eval_jaxpr/ppermute | solution.py:16
  250.6 11.8 %collective-permute-start = (bf16[64,2048]{1,0:T(8,128)(2,1)S(1)}, bf16[64,2048]{1,0:T(8,128)(2,1)S(1)}, u32[]{:S(2)}, u32[]{:S(2)}) collective-permute-start(bf16[64,2048]{1,0:T(8,128)(2,1)S(1)} %get-tuple-element.430), channel_id=1, source_target_pairs={{124,0},{0,4},{4,8},{8,12},{12,16},{16,20},{20,24},{24,28},{28,32}... | collective-permute-start | bytes 786440 | tf_op jit(solution)/shard_map/while/body/eval_jaxpr/ppermute | solution.py:16
  268.3 12.0 %collective-permute-start = (bf16[64,2048]{1,0:T(8,128)(2,1)S(1)}, bf16[64,2048]{1,0:T(8,128)(2,1)S(1)}, u32[]{:S(2)}, u32[]{:S(2)}) collective-permute-start(bf16[64,2048]{1,0:T(8,128)(2,1)S(1)} %get-tuple-element.430), channel_id=1, source_target_pairs={{124,0},{0,4},{4,8},{8,12},{12,16},{16,20},{20,24},{24,28},{28,32}... | collective-permute-start | bytes 786440 | tf_op jit(solution)/shard_map/while/body/eval_jaxpr/ppermute | solution.py:16
  286.2 11.1 %collective-permute-start = (bf16[64,2048]{1,0:T(8,128)(2,1)S(1)}, bf16[64,2048]{1,0:T(8,128)(2,1)S(1)}, u32[]{:S(2)}, u32[]{:S(2)}) collective-permute-start(bf16[64,2048]{1,0:T(8,128)(2,1)S(1)} %get-tuple-element.430), channel_id=1, source_target_pairs={{124,0},{0,4},{4,8},{8,12},{12,16},{16,20},{20,24},{24,28},{28,32}... | collective-permute-start | bytes 786440 | tf_op jit(solution)/shard_map/while/body/eval_jaxpr/ppermute | solution.py:16
  303.2 10.2 %collective-permute-start = (bf16[64,2048]{1,0:T(8,128)(2,1)S(1)}, bf16[64,2048]{1,0:T(8,128)(2,1)S(1)}, u32[]{:S(2)}, u32[]{:S(2)}) collective-permute-start(bf16[64,2048]{1,0:T(8,128)(2,1)S(1)} %get-tuple-element.430), channel_id=1, source_target_pairs={{124,0},{0,4},{4,8},{8,12},{12,16},{16,20},{20,24},{24,28},{28,32}... | collective-permute-start | bytes 786440 | tf_op jit(solution)/shard_map/while/body/eval_jaxpr/ppermute | solution.py:16
  350.3 9.5 %collective-permute-start = (bf16[64,2048]{1,0:T(8,128)(2,1)S(1)}, bf16[64,2048]{1,0:T(8,128)(2,1)S(1)}, u32[]{:S(2)}, u32[]{:S(2)}) collective-permute-start(bf16[64,2048]{1,0:T(8,128)(2,1)S(1)} %get-tuple-element.430), channel_id=1, source_target_pairs={{124,0},{0,4},{4,8},{8,12},{12,16},{16,20},{20,24},{24,28},{28,32}... | collective-permute-start | bytes 786440 | tf_op jit(solution)/shard_map/while/body/eval_jaxpr/ppermute | solution.py:16
  443.2 9.5 %collective-permute-start = (bf16[64,2048]{1,0:T(8,128)(2,1)S(1)}, bf16[64,2048]{1,0:T(8,128)(2,1)S(1)}, u32[]{:S(2)}, u32[]{:S(2)}) collective-permute-start(bf16[64,2048]{1,0:T(8,128)(2,1)S(1)} %get-tuple-element.430), channel_id=1, source_target_pairs={{124,0},{0,4},{4,8},{8,12},{12,16},{16,20},{20,24},{24,28},{28,32}... | collective-permute-start | bytes 786440 | tf_op jit(solution)/shard_map/while/body/eval_jaxpr/ppermute | solution.py:16
  474.2 10.5 %collective-permute-start = (bf16[64,2048]{1,0:T(8,128)(2,1)S(1)}, bf16[64,2048]{1,0:T(8,128)(2,1)S(1)}, u32[]{:S(2)}, u32[]{:S(2)}) collective-permute-start(bf16[64,2048]{1,0:T(8,128)(2,1)S(1)} %get-tuple-element.430), channel_id=1, source_target_pairs={{124,0},{0,4},{4,8},{8,12},{12,16},{16,20},{20,24},{24,28},{28,32}... | collective-permute-start | bytes 786440 | tf_op jit(solution)/shard_map/while/body/eval_jaxpr/ppermute | solution.py:16
  490.6 11.6 %collective-permute-start = (bf16[64,2048]{1,0:T(8,128)(2,1)S(1)}, bf16[64,2048]{1,0:T(8,128)(2,1)S(1)}, u32[]{:S(2)}, u32[]{:S(2)}) collective-permute-start(bf16[64,2048]{1,0:T(8,128)(2,1)S(1)} %get-tuple-element.430), channel_id=1, source_target_pairs={{124,0},{0,4},{4,8},{8,12},{12,16},{16,20},{20,24},{24,28},{28,32}... | collective-permute-start | bytes 786440 | tf_op jit(solution)/shard_map/while/body/eval_jaxpr/ppermute | solution.py:16
  508.2 12.2 %collective-permute-start = (bf16[64,2048]{1,0:T(8,128)(2,1)S(1)}, bf16[64,2048]{1,0:T(8,128)(2,1)S(1)}, u32[]{:S(2)}, u32[]{:S(2)}) collective-permute-start(bf16[64,2048]{1,0:T(8,128)(2,1)S(1)} %get-tuple-element.430), channel_id=1, source_target_pairs={{124,0},{0,4},{4,8},{8,12},{12,16},{16,20},{20,24},{24,28},{28,32}... | collective-permute-start | bytes 786440 | tf_op jit(solution)/shard_map/while/body/eval_jaxpr/ppermute | solution.py:16
  528.1 11.2 %all-to-all-start = ((f32[32,1,1024]{2,1,0:T(1,128)}), f32[32,1,1024]{2,1,0:T(1,128)S(1)}, u32[]{:S(2)}, u32[]{:S(2)}) async-start(f32[32,1,1024]{2,1,0:T(1,128)} %reshape.462), calls=%async_computation | async-start | bytes 262144 | tf_op jit(solution)/shard_map/all_to_all | solution.py:132
  550.1 65.9 %all-to-all-start.2 = ((bf16[32,64,2048]{2,1,0:T(8,128)(2,1)}), bf16[32,64,2048]{2,1,0:T(8,128)(2,1)}, u32[]{:S(2)}, u32[]{:S(2)}) async-start(bf16[32,64,2048]{2,1,0:T(8,128)(2,1)} %get-tuple-element.298), calls=%async_computation.2 | async-start | bytes 16777216 | tf_op jit(solution)/shard_map/all_to_all | solution.py:129
  555.1 301.4 %all-gather.2.cloned.1.call-start = ((), (), s32[]{:S(2)}) async-start(), calls=%async_computation.4 | async-start | bytes 8650752 | tf_op jit(solution)/shard_map/all_gather | solution.py:137
  635.3 288.9 %reduce-scatter.2.cloned.1.call-start = ((), (), s32[]{:S(2)}) async-start(), calls=%async_computation.5 | async-start | bytes 2621440 | tf_op jit(solution)/shard_map/reduce_scatter | solution.py:141
  (19 other events, 1004.4 us)
Sparse Core Ops, SparseCore 0:
  635.4 221.0 all-gather.1
  865.8 58.2 reduce-scatter.1
where the time goes:
time: 933 us; the launch traced here: 931 us
  waiting for transfers between devices  586 us (63%)
  local copies, waits for them, and re-layouts  124 us (13%)
  matrix products  118 us (13%)
  other arithmetic  44.4 us (5%)
  loops' own time  20.9 us (2%)
  between operations  14.3 us (2%)
  starting transfers between devices  13.5 us (1%)
  blocking collectives  10.7 us (1%)
    ppermute x31, waiting for transfers between devices, from_behind(): return lax.ppermute(block, axis, route)  243 us
    all_gather x1, waiting for transfers between devices, shards(): lax.all_gather(attended, 'ctx', axis=0, tiled=True)  221 us
    dot_general x32, matrix products, partial_tile(): jnp.einsum('gjrk,kgd->rgjd', weights.astype(jnp.bfloat16), value_rows, pr...  65.6 us
    reduce_scatter x1, waiting for transfers between devices, shards(): lax.psum_scatter(head_terms.astype(jnp.bfloat16), 'tp', scatter_dimension...  58.5 us
    all_to_all x1, waiting for transfers between devices, shards(): lax.all_to_all(outputs.astype(jnp.float32), 'ctx', split_axis=0, concat_a...  57.3 us
    reduce_sum x32, other arithmetic, partial_tile(): totals = jnp.sum(weights, axis=3)  37.1 us
    dot_general x32, matrix products, partial_tile(): jnp.einsum('rgjd,kgd->gjrk', grouped, key_rows, preferred_element_type=jn...  34.3 us
    gather x32, local copies, waits for them, and re-layouts, query_info(): return (position, new_docs[position // BLK])  24.9 us
  transfers between devices with their start and end apart: 35, of which 35 were waited for; matrix products, arithmetic and copies ran while one was open for 6% of the time, Pallas kernels for 0%

commit v1 on v0

v1 whole, which is shorter than its diff:
```python
import functools
import jax, jax.numpy as jnp
from jax import lax
from jax.experimental import pallas as pl
from jax.experimental.pallas import tpu as pltpu
from jax.sharding import PartitionSpec as P

HD=128; BLK=128; NEG=-1e30
SCALE=HD**-0.5
L2E=1.4426950408889634
ROWS=64; HEADS=16; CR=1024; HALF=CR+ROWS; MEM=2*HALF
SUB=1024

def attn_kernel(cdocs, ndocs, tiles, place, q_ref, kv_ref, o_ref, st_ref, q_s, m_s, l_s, acc_s, lst, *, nb):
    g = pl.program_id(0)
    c = place[0]
    y = c % 4
    src = g * 4 + y
    members = [c - y + i for i in range(4)]
    tq = tiles[src]
    qd = ndocs[tq // 2]
    nrow = ROWS*HEADS
    for h in range(HEADS):
        q_s[h*ROWS:(h+1)*ROWS, :] = q_ref[0, :, h*HD:(h+1)*HD]
    m_s[...] = jnp.full_like(m_s, NEG)
    l_s[...] = jnp.zeros_like(l_s)
    acc_s[...] = jnp.zeros_like(acc_s)
    n = jnp.int32(0)
    for mi, c in enumerate(members):
        def add(b, n):
            ok = cdocs[c*8 + b] == qd
            lst[n] = mi*MEM + b*BLK
            return n + ok.astype(jnp.int32)
        n = lax.fori_loop(0, 8, add, n)

    def slow_step(kc, vc, mask_fn):
        for t in range(nrow//SUB):
            r = pl.ds(t*SUB, SUB)
            s = lax.dot_general(q_s[r, :], kc, (((1,),(1,)),((),())), preferred_element_type=jnp.float32)
            if mask_fn is not None:
                s = mask_fn(s)
            w = s.shape[1]//128
            mx = s[:, :128]
            for i in range(1, w):
                mx = jnp.maximum(mx, s[:, i*128:(i+1)*128])
            mx = jnp.max(mx, axis=1, keepdims=True)
            m_old = m_s[r, :]
            m_new = jnp.maximum(m_old, mx)
            alpha = jnp.exp2((m_old - m_new)*(SCALE*L2E))
            p = [jnp.exp2((s[:, i*128:(i+1)*128] - m_new)*(SCALE*L2E)) for i in range(w)]
            ps = p[0]
            for i in range(1, w):
                ps = ps + p[i]
            l_s[r, :] = l_s[r, :]*alpha + ps
            m_s[r, :] = m_new
            pb = jnp.concatenate([x.astype(jnp.bfloat16) for x in p], axis=1)
            acc_s[r, :] = acc_s[r, :]*alpha + jnp.dot(pb, vc, preferred_element_type=jnp.float32)


    def peak(kc, mask_fn):
        for t in range(nrow//SUB):
            r = pl.ds(t*SUB, SUB)
            s = lax.dot_general(q_s[r, :], kc, (((1,),(1,)),((),())), preferred_element_type=jnp.float32)
            if mask_fn is not None:
                s = mask_fn(s)
            w = s.shape[1]//128
            mx = s[:, :128]
            for i in range(1, w):
                mx = jnp.maximum(mx, s[:, i*128:(i+1)*128])
            m_s[r, :] = jnp.broadcast_to(jnp.max(mx, axis=1, keepdims=True), (SUB, 128))

    def step(kc, vc, mask_fn):
        for t in range(nrow//SUB):
            r = pl.ds(t*SUB, SUB)
            s = lax.dot_general(q_s[r, :], kc, (((1,),(1,)),((),())), preferred_element_type=jnp.float32)
            if mask_fn is not None:
                s = mask_fn(s)
            w = s.shape[1]//128
            m = m_s[r, :]
            p = [jnp.exp2((s[:, i*128:(i+1)*128] - m)*(SCALE*L2E)) for i in range(w)]
            ps = p[0]
            for i in range(1, w):
                ps = ps + p[i]
            l_s[r, :] = l_s[r, :] + ps
            pb = jnp.concatenate([x.astype(jnp.bfloat16) for x in p], axis=1)
            acc_s[r, :] = acc_s[r, :] + jnp.dot(pb, vc, preferred_element_type=jnp.float32)

    def at(off, rows=BLK):
        return kv_ref[pl.ds(pl.multiple_of(off, 64), rows), :]

    def chunks(step):
        def chunk(base, size):
            offs = [lst[base + j] for j in range(size)]
            kc = jnp.concatenate([at(o) for o in offs], axis=0)
            vc = jnp.concatenate([at(o + HALF) for o in offs], axis=0)
            step(kc, vc, None)
        def body(i, _):
            chunk(i*nb, nb)
            return 0
        lax.fori_loop(0, n // nb, body, 0)
        size = nb // 2
        while size >= 1:
            @pl.when((n // size) % 2 == 1)
            def _(size=size):
                chunk((n // (2*size))*(2*size), size)
            size //= 2
    kcs = []; vcs = []
    newlims = []
    for mi, c in enumerate(members):
        tk = tiles[c]
        same_doc = ndocs[tk // 2] == qd
        full_ok = same_doc & (tk < tq)
        diag = tk == tq
        newlims.append((jnp.where(full_ok, 1 << 20, jnp.where(diag, 0, -1)), jnp.where(diag, 1, 0)))
        kcs.append(kv_ref[mi*MEM + CR: mi*MEM + HALF, :])
        vcs.append(kv_ref[mi*MEM + HALF + CR: (mi+1)*MEM, :])
    kc = jnp.concatenate(kcs, axis=0); vc = jnp.concatenate(vcs, axis=0)
    any_new = functools.reduce(jnp.logical_or, [lim >= 0 for lim, _ in newlims])
    def mask(s):
        row = lax.broadcasted_iota(jnp.int32, (SUB, 128), 0) % ROWS
        lane = lax.broadcasted_iota(jnp.int32, (SUB, 128), 1)
        out = []
        for a in range(2):
            (b0, d0), (b1, d1) = newlims[2*a], newlims[2*a+1]
            lo = row*d0 + b0
            hi = row*d1 + b1
            ok = lane <= jnp.where(lane < ROWS, lo, hi + ROWS)
            k0 = a*128
            out.append(jnp.where(ok, s[:, k0:k0+128], NEG))
        return jnp.concatenate(out, axis=1)
    @pl.when(n > 0)
    def _():
        peak(at(lst[0]), None)
    @pl.when((n == 0) & any_new)
    def _():
        peak(kc, mask)
    chunks(step)
    @pl.when(any_new)
    def _():
        step(kc, vc, mask)
    @pl.when(jnp.logical_not(jnp.max(l_s[...]) < 1e30))
    def _():
        m_s[...] = jnp.full_like(m_s, NEG)
        l_s[...] = jnp.zeros_like(l_s)
        acc_s[...] = jnp.zeros_like(acc_s)
        chunks(slow_step)
        @pl.when(any_new)
        def _():
            slow_step(kc, vc, mask)
    lane = lax.broadcasted_iota(jnp.int32, (ROWS, 128), 1)
    st = jnp.full((ROWS, 128), NEG, jnp.float32)
    for h in range(HEADS):
        r = pl.ds(h*ROWS, ROWS)
        l = jnp.sum(l_s[r, :], axis=1, keepdims=True)
        l = jnp.maximum(l, 1e-30)
        o_ref[0, :, h*HD:(h+1)*HD] = (acc_s[r, :] / l).astype(jnp.bfloat16)
        lse = m_s[r, :]*SCALE + jnp.log(l)
        st = jnp.where(lane == h, lse, st)
    st_ref[0] = st

def attention(qg, kvg, cdocs, ndocs, tiles, place, nb=4):
    nrow = ROWS*HEADS
    return pl.pallas_call(
        functools.partial(attn_kernel, nb=nb),
        grid_spec=pltpu.PrefetchScalarGridSpec(
            num_scalar_prefetch=4, grid=(8,),
            in_specs=[pl.BlockSpec((1, ROWS, HEADS*HD), lambda g, *_: (g, 0, 0)),
                      pl.BlockSpec((4*MEM, HD), lambda g, *_: (0, 0))],
            out_specs=[pl.BlockSpec((1, ROWS, HEADS*HD), lambda g, *_: (g, 0, 0)),
                       pl.BlockSpec((1, ROWS, 128), lambda g, *_: (g, 0, 0))],
            scratch_shapes=[pltpu.VMEM((nrow, HD), jnp.bfloat16), pltpu.VMEM((nrow, 128), jnp.float32),
                            pltpu.VMEM((nrow, 128), jnp.float32), pltpu.VMEM((nrow, HD), jnp.float32),
                            pltpu.SMEM((40,), jnp.int32)]),
        out_shape=[jax.ShapeDtypeStruct((8, ROWS, HEADS*HD), jnp.bfloat16),
                   jax.ShapeDtypeStruct((8, ROWS, 128), jnp.float32)],
        compiler_params=pltpu.CompilerParams(vmem_limit_bytes=48 << 20),
        name="attention",
    )(cdocs, ndocs, tiles, place, qg, kvg)


MESH = pl.DeviceIdType.MESH


def coords():
    c = lax.axis_index("ctx")
    return c // 16, (c // 4) % 4, c % 4


def ctx_of(z, x, y):
    return z * 16 + x * 4 + y


def send(src, dst, sems, i, device):
    copy = pltpu.make_async_remote_copy(
        src_ref=src, dst_ref=dst, send_sem=sems[0].at[i], recv_sem=sems[1].at[i],
        device_id=device, device_id_type=MESH)
    copy.start()
    return copy


def arrive(ref, sems, i, device):
    pltpu.make_async_remote_copy(
        src_ref=ref, dst_ref=ref, send_sem=sems[0].at[i], recv_sem=sems[1].at[i],
        device_id=device, device_id_type=MESH).wait_recv()


def greet(peers):
    barrier = pltpu.get_barrier_semaphore()
    for device in peers:
        pl.semaphore_signal(barrier, inc=1, device_id=device, device_id_type=MESH)
    pl.semaphore_wait(barrier, len(peers))


def gather_kernel(q, ck, cv, nk, nv, qg, kvg, ssem, rsem, lsem):
    z, x, y = coords()
    sems = (ssem, rsem)
    zp = 1 - z
    xr, xl, yr, yl = (x + 1) % 4, (x + 3) % 4, (y + 1) % 4, (y + 3) % 4
    x2, y2 = (x + 2) % 4, (y + 2) % 4
    dev = lambda z, x, y: {"ctx": ctx_of(z, x, y)}
    to_yr, to_yl, to_xr, to_xl, to_z = dev(z, x, yr), dev(z, x, yl), dev(z, xr, y), dev(z, xl, y), dev(zp, x, y)
    greet([to_yr, to_yl, to_xr, to_xl, to_z])
    slot = lambda z, x: z * 4 + x
    me = slot(z, x)
    out = []
    out.append(send(q, qg.at[me], sems, 0, to_z))
    pieces = [(ck, 0, CR), (nk, CR, ROWS), (cv, HALF, CR), (nv, HALF + CR, ROWS)]
    for i in (0, 1, 2, 3):
        src, off, n = pieces[i]
        out.append(send(src, kvg.at[y, pl.ds(off, n)], sems, 1 + i, to_yr))
    for i in (2, 3, 0, 1):
        src, off, n = pieces[i]
        out.append(send(src, kvg.at[y, pl.ds(off, n)], sems, 5 + i, to_yl))
    out.append(send(q, qg.at[me], sems, 9, to_xr))
    out.append(send(q, qg.at[me], sems, 10, to_xl))
    locs = [pltpu.make_async_copy(q, qg.at[me], lsem.at[0])]
    for i, (src, off, n) in enumerate(pieces):
        locs.append(pltpu.make_async_copy(src, kvg.at[y, pl.ds(off, n)], lsem.at[1 + i]))
    for cp in locs:
        cp.start()
    other = slot(zp, x)
    arrive(qg.at[other], sems, 0, to_z)
    out.append(send(qg.at[other], qg.at[other], sems, 11, to_xr))
    out.append(send(qg.at[other], qg.at[other], sems, 12, to_xl))
    lo, hi = pl.ds(0, 32), pl.ds(32, 32)
    arrive(qg.at[slot(z, xl)], sems, 9, to_xl)
    out.append(send(qg.at[slot(z, xl), lo], qg.at[slot(z, xl), lo], sems, 13, to_xr))
    arrive(qg.at[slot(z, xr)], sems, 10, to_xr)
    out.append(send(qg.at[slot(z, xr), hi], qg.at[slot(z, xr), hi], sems, 14, to_xl))
    arrive(kvg.at[yl, pl.ds(0, CR)], sems, 1, to_yl)
    arrive(kvg.at[yl, pl.ds(CR, ROWS)], sems, 2, to_yl)
    kh, vh = pl.ds(0, HALF), pl.ds(HALF, HALF)
    out.append(send(kvg.at[yl, kh], kvg.at[yl, kh], sems, 17, to_yr))
    arrive(kvg.at[yr, pl.ds(HALF, CR)], sems, 7, to_yr)
    arrive(kvg.at[yr, pl.ds(HALF + CR, ROWS)], sems, 8, to_yr)
    out.append(send(kvg.at[yr, vh], kvg.at[yr, vh], sems, 18, to_yl))
    arrive(qg.at[slot(zp, xl)], sems, 11, to_xl)
    out.append(send(qg.at[slot(zp, xl), lo], qg.at[slot(zp, xl), lo], sems, 15, to_xr))
    arrive(qg.at[slot(zp, xr)], sems, 12, to_xr)
    out.append(send(qg.at[slot(zp, xr), hi], qg.at[slot(zp, xr), hi], sems, 16, to_xl))
    arrive(kvg.at[yl, pl.ds(HALF, CR)], sems, 3, to_yl)
    arrive(kvg.at[yl, pl.ds(HALF + CR, ROWS)], sems, 4, to_yl)
    arrive(kvg.at[yr, pl.ds(0, CR)], sems, 5, to_yr)
    arrive(kvg.at[yr, pl.ds(CR, ROWS)], sems, 6, to_yr)
    arrive(qg.at[slot(z, x2), lo], sems, 13, to_xl)
    arrive(qg.at[slot(z, x2), hi], sems, 14, to_xr)
    arrive(qg.at[slot(zp, x2), lo], sems, 15, to_xl)
    arrive(qg.at[slot(zp, x2), hi], sems, 16, to_xr)
    arrive(kvg.at[y2, kh], sems, 17, to_yl)
    arrive(kvg.at[y2, vh], sems, 18, to_yr)
    for cp in locs:
        cp.wait()
    for cp in out:
        cp.wait_send()


def gather(q, ck, cv, nk, nv):
    anywhere = pl.BlockSpec(memory_space=pl.ANY)
    return pl.pallas_call(
        gather_kernel,
        in_specs=[anywhere] * 5,
        out_specs=[anywhere] * 2,
        out_shape=[jax.ShapeDtypeStruct((8, ROWS, HEADS * HD), jnp.bfloat16),
                   jax.ShapeDtypeStruct((4, MEM, HD), jnp.bfloat16)],
        scratch_shapes=[pltpu.SemaphoreType.DMA((19,)), pltpu.SemaphoreType.DMA((19,)), pltpu.SemaphoreType.DMA((5,))],
        compiler_params=pltpu.CompilerParams(collective_id=0, has_side_effects=True),
        name="gather",
    )(q, ck, cv, nk, nv)


def project_kernel(o, st, w, wp, out, part, stp, attg, w_s, tx, rx, acc, zt, zr,
                   psem, qsem, gs, gr, cs, cr, zs, zrs, lsem):
    z, x, y = coords()
    t = lax.axis_index("tp")
    h, k = t // 2, t % 2
    dev = lambda z, x, y: {"ctx": ctx_of(z, x, y)}
    zdev = lambda b, zh: {"ctx": ctx_of(b, x, y), "tp": zh * 2 + k}
    zp = 1 - z
    xr, xl, yr, yl = (x + 1) % 4, (x + 3) % 4, (y + 1) % 4, (y + 3) % 4
    group = [(dz, dx) for dz in (0, 1) for dx in range(4) if (dz, dx) != (0, 0)]
    there = lambda dz, dx: ((z + dz) % 2, (x + dx) % 4)
    core = {"tp": h * 2 + 1 - k}
    to_yr, to_yl, to_xr, to_xl = dev(z, x, yr), dev(z, x, yl), dev(z, xr, y), dev(z, xl, y)
    greet([dev(*there(dz, dx), y) for dz, dx in group] + [to_yr, to_yl, core, zdev(0, 1 - h), zdev(1, 1 - h)])

    me = z * 4 + x
    outs = []
    order = sorted(group, key=lambda d: -(d[0] + (d[1] != 0) + (d[1] == 2)))
    for dz, dx in order:
        zz, xx = there(dz, dx)
        i = dz * 4 + dx
        outs.append(send(st.at[zz * 4 + xx], stp.at[me], (psem.at[1], qsem.at[1]), i, dev(zz, xx, y)))
        outs.append(send(o.at[zz * 4 + xx], part.at[me], (psem.at[0], qsem.at[0]), i, dev(zz, xx, y)))
    own = [pltpu.make_async_copy(o.at[me], part.at[me], lsem.at[0]),
           pltpu.make_async_copy(st.at[me], stp.at[me], lsem.at[1])]
    weights = [pltpu.make_async_copy(w, w_s.at[z], lsem.at[2]),
               pltpu.make_async_copy(wp, w_s.at[zp], lsem.at[3])]
    for cp in own + weights:
        cp.start()
    for cp in own:
        cp.wait()
    for dz, dx in order:
        zz, xx = (z + 2 - dz) % 2, (x + 4 - dx) % 4
        i = dz * 4 + dx
        arrive(stp.at[zz * 4 + xx], (psem.at[1], qsem.at[1]), i, dev(zz, xx, y))
        arrive(part.at[zz * 4 + xx], (psem.at[0], qsem.at[0]), i, dev(zz, xx, y))

    largest = stp[0]
    for c in range(1, 8):
        largest = jnp.maximum(largest, stp[c])
    e = [jnp.exp(stp[c] - largest) for c in range(8)]
    total = e[0]
    for c in range(1, 8):
        total = total + e[c]
    inverse = 1.0 / total
    e = [a * inverse for a in e]
    mine = x * 4 + y
    for head in range(HEADS):
        cols = pl.ds(head * HD, HD)
        a = jnp.zeros((ROWS, HD), jnp.float32)
        for c in range(8):
            a = a + e[c][:, head:head + 1] * part[c, :, cols].astype(jnp.float32)
        attg[head // 8, mine, :, (head % 8) * HD:(head % 8 + 1) * HD] = a.astype(jnp.bfloat16)

    lo, hi = pl.ds(0, 32), pl.ds(32, 32)
    slot = lambda x, y: x * 4 + y

    def block(hf, a, b):
        if hf == 0:
            return attg.at[0, slot((x + a) % 4, (y + b) % 4)]
        return attg.at[1, slot((x + b) % 4, (y + a) % 4)]

    def ways(hf, stage):
        return (to_xr, to_xl) if (hf == 0) == (stage == 0) else (to_yr, to_yl)

    def both(hf, stage, a, b, i):
        right, left = ways(hf, stage)
        ref = block(hf, a, b)
        outs.append(send(ref, ref, (gs.at[hf], gr.at[hf]), i, right))
        outs.append(send(ref, ref, (gs.at[hf], gr.at[hf]), i + 1, left))

    def relay(hf, stage, a, b, i):
        right, left = ways(hf, stage)
        d = (lambda n: (n, 0)) if stage == 0 else (lambda n: (a, n))
        ref = block(hf, *d(3))
        arrive(ref, (gs.at[hf], gr.at[hf]), i, left)
        outs.append(send(ref.at[lo], ref.at[lo], (gs.at[hf], gr.at[hf]), i + 2, right))
        ref = block(hf, *d(1))
        arrive(ref, (gs.at[hf], gr.at[hf]), i + 1, right)
        outs.append(send(ref.at[hi], ref.at[hi], (gs.at[hf], gr.at[hf]), i + 3, left))

    def last(hf, stage, a, b, i):
        right, left = ways(hf, stage)
        ref = block(hf, 2, 0) if stage == 0 else block(hf, a, 2)
        arrive(ref.at[lo], (gs.at[hf], gr.at[hf]), i + 2, left)
        arrive(ref.at[hi], (gs.at[hf], gr.at[hf]), i + 3, right)

    for hf in (0, 1):
        both(hf, 0, 0, 0, 0)
    for hf in (0, 1):
        both(hf, 1, 0, 0, 4)
    for hf in (0, 1):
        relay(hf, 0, 0, 0, 0)
        both(hf, 1, 3, 0, 8)
        both(hf, 1, 1, 0, 12)
    for hf in (0, 1):
        relay(hf, 1, 0, 0, 4)
    for hf in (0, 1):
        last(hf, 0, 0, 0, 0)
        both(hf, 1, 2, 0, 16)
    for a, i in ((3, 8), (1, 12), (2, 16)):
        for hf in (0, 1):
            relay(hf, 1, a, 0, i)
    for a, i in ((0, 4), (3, 8), (1, 12), (2, 16)):
        for hf in (0, 1):
            last(hf, 1, a, 0, i)
    for cp in weights:
        cp.wait()

    def rows_of(group, b):
        lhs = [jnp.concatenate([attg[hf, group * 4 + i] for i in range(4)], axis=0) for hf in (0, 1)]
        return (jnp.dot(lhs[0], w_s[b, :1024, :], preferred_element_type=jnp.float32)
                + jnp.dot(lhs[1], w_s[b, 1024:, :], preferred_element_type=jnp.float32))

    for i in (0, 1):
        for b in (0, 1):
            tx[i, b] = rows_of(2 * (1 - k) + i, b).astype(jnp.bfloat16)
        outs.append(send(tx.at[i], rx.at[i], (cs, cr), i, core))
    for i in (0, 1):
        for b in (0, 1):
            acc[i, b] = rows_of(2 * k + i, b)
    mine_at = lambda b: (h == z) & (b == z)
    for i in (0, 1):
        arrive(rx.at[i], (cs, cr), i, core)
        for b in (0, 1):
            zt[b, i] = (acc[i, b] + rx[i, b].astype(jnp.float32)).astype(jnp.bfloat16)

            @pl.when(jnp.logical_not(mine_at(b)))
            def _():
                send(zt.at[b, i], zr.at[h, i], (zs, zrs.at[h]), i * 2 + b, zdev(b, z))

            @pl.when(mine_at(b))
            def _():
                zr[h, i] = zt[b, i]
    for i in (0, 1):
        for s in (0, 1):
            @pl.when(jnp.logical_not((s == h) & (z == h)))
            def _():
                pltpu.make_async_remote_copy(
                    src_ref=zr.at[s, i], dst_ref=zr.at[s, i], send_sem=zs.at[0], recv_sem=zrs.at[s, i * 2 + z],
                    device_id=zdev(h, s), device_id_type=MESH).wait_recv()
        out[pl.ds(i * 256, 256), :] = (zr[0, i].astype(jnp.float32) + zr[1, i].astype(jnp.float32)).astype(jnp.bfloat16)
    for i in (0, 1):
        for b in (0, 1):
            @pl.when(jnp.logical_not(mine_at(b)))
            def _():
                pltpu.make_async_remote_copy(
                    src_ref=zt.at[b, i], dst_ref=zt.at[b, i], send_sem=zs.at[i * 2 + b], recv_sem=zrs.at[0, 0],
                    device_id=zdev(b, z), device_id_type=MESH).wait_send()
    for cp in outs:
        cp.wait_send()


def project(o, st, w, wp):
    anywhere = pl.BlockSpec(memory_space=pl.ANY)
    dma = pltpu.SemaphoreType.DMA
    bf = jnp.bfloat16
    return pl.pallas_call(
        project_kernel,
        in_specs=[anywhere] * 4,
        out_specs=pl.BlockSpec(memory_space=pltpu.VMEM),
        out_shape=jax.ShapeDtypeStruct((512, 512), bf),
        scratch_shapes=[
            pltpu.VMEM((8, ROWS, HEADS * HD), bf), pltpu.VMEM((8, ROWS, 128), jnp.float32),
            pltpu.VMEM((2, 16, ROWS, 1024), bf), pltpu.VMEM((2, 2048, 512), bf),
            pltpu.VMEM((2, 2, 256, 512), bf), pltpu.VMEM((2, 2, 256, 512), bf),
            pltpu.VMEM((2, 2, 256, 512), jnp.float32),
            pltpu.VMEM((2, 2, 256, 512), bf), pltpu.VMEM((2, 2, 256, 512), bf),
            dma((2, 8)), dma((2, 8)), dma((2, 20)), dma((2, 20)), dma((2,)), dma((2,)), dma((4,)), dma((2, 4)), dma((4,)),
        ],
        compiler_params=pltpu.CompilerParams(collective_id=1, has_side_effects=True, vmem_limit_bytes=48 << 20),
        name="project",
    )(o, st, w, wp)


def shards(new_queries, new_keys, new_values, cache_keys, cache_values, out_weight, cache_docs, new_docs, slot_tile):
    other = lax.ppermute(out_weight, "ctx", [(i, i ^ 16) for i in range(32)])
    qg, kvg = gather(new_queries, cache_keys, cache_values, new_keys, new_values)
    c = lax.axis_index("ctx")
    place = jnp.reshape(c, (1,)).astype(jnp.int32)
    o, st = attention(qg, kvg.reshape(4 * MEM, HD), cache_docs, new_docs, slot_tile, place)
    return project(o, st, out_weight, other)


def solution(mesh):
    return jax.shard_map(
        shards,
        mesh=mesh,
        in_specs=(
            P("ctx", "tp"),
            P("ctx", "tp"),
            P("ctx", "tp"),
            P("ctx", "tp"),
            P("ctx", "tp"),
            P("tp", "ctx"),
            P(),
            P(),
            P(),
        ),
        out_specs=P("tp", "ctx"),
        check_vma=False,
    )
```

time: 933 us -> 184 us (0.20)
  waiting for transfers between devices: 586 us -> 0.01 us
  Pallas kernels: 0 us -> 175 us
  local copies, waits for them, and re-layouts: 124 us -> 5.71 us
  matrix products: 118 us -> 0 us
  other arithmetic: 44.4 us -> 0 us
  loops' own time: 20.9 us -> 0 us
  between operations: 14.3 us -> 0.05 us
  starting transfers between devices: 13.5 us -> 2.47 us
  blocking collectives: 10.7 us -> 0 us
    ppermute x31 -> x1, waiting for transfers between devices: 243 us -> 0.01 us  [shards(): other = lax.ppermute(out_weight, 'ctx', [(i, i ^ 16) for i in range(32)])]
    all_gather x1 -> x0, waiting for transfers between devices: 221 us -> none  [shards(): lax.all_gather(attended, 'ctx', axis=0, tiled=True)]
    pallas_call x0 -> x3, Pallas kernels: none -> 175 us  [the longest x1 74.5 us: project(): pl.pallas_call(project_kernel, in_specs=[anywhere] * 4, out_specs=pl.Bloc...]
    dot_general x66 -> x0, matrix products: 118 us -> none  [the longest x32 65.6 us: partial_tile(): jnp.einsum('gjrk,kgd->rgjd', weights.astype(jnp.bfloat16), value_rows, pr...]
    all_to_all x2 -> x0, waiting for transfers between devices: 63.5 us -> none  [the longest x1 57.3 us: shards(): lax.all_to_all(outputs.astype(jnp.float32), 'ctx', split_axis=0, concat_a...]
    reduce_scatter x1 -> x0, waiting for transfers between devices: 58.5 us -> none  [shards(): lax.psum_scatter(head_terms.astype(jnp.bfloat16), 'tp', scatter_dimension...]
    dynamic_update_slice x64 -> x0, local copies, waits for them, and re-layouts: 42.7 us -> none  [the longest x32 22.7 us: visit(): outputs = lax.dynamic_update_index_in_dim(outputs, partial_value, source, 0)]
    reduce_sum x33 -> x0, other arithmetic: 37.2 us -> none  [the longest x32 37.1 us: partial_tile(): totals = jnp.sum(weights, axis=3)]
  transfers between devices with their start and end apart: 35 -> 1, of which waited for: 35 -> 0; matrix products, arithmetic and copies ran while one was open for 6% -> 0% of each run, Pallas kernels for 0% -> 55%
where the time goes in v1:
time: 184 us; the launch traced here: 183 us
  Pallas kernels  175 us (95%)
  local copies, waits for them, and re-layouts  5.71 us (3%)
  starting transfers between devices  2.47 us (1%)
    pallas_call x1, Pallas kernels, project(): pl.pallas_call(project_kernel, in_specs=[anywhere] * 4, out_specs=pl.Bloc...  74.5 us
    pallas_call x1, Pallas kernels, gather(): pl.pallas_call(gather_kernel, in_specs=[anywhere] * 5, out_specs=[anywher...  65.3 us
    pallas_call x1, Pallas kernels, attention(): pl.pallas_call(functools.partial(attn_kernel, nb=nb), grid_spec=pltpu.Pre...  35.4 us
    unnamed x13, local copies, waits for them, and re-layouts  5.71 us
  transfers between devices with their start and end apart: 1, of which 0 were waited for; matrix products, arithmetic and copies ran while one was open for 0% of the time, Pallas kernels for 55%

profile of v1, /device:TPU:1, one launch (start us, length us, event | category | flops | bytes accessed | tf_op | source)
XLA Modules:
  0.0 183.4 jit_solution(9818561565151206515)
XLA Ops:
  0.0 2.5 %collective-permute-start = (bf16[2048,512]{1,0:T(8,128)(2,1)}, bf16[2048,512]{1,0:T(8,128)(2,1)S(1)}, u32[]{:S(2)}, u32[]{:S(2)}) collective-permute-start(bf16[2048,512]{1,0:T(8,128)(2,1)} %w.1), channel_id=1, source_target_pairs={{0,64},{4,68},{8,72},{12,76},{16,80},{20,84},{24,88},{28,92},{32,9... | collective-permute-start | bytes 6291464 | tf_op jit(solution)/shard_map/ppermute | solution.py:467
  2.5 65.3 %gather.1 = (bf16[8,64,2048]{2,1,0:T(8,128)(2,1)}, bf16[4,2176,128]{2,1,0:T(8,128)(2,1)}) custom-call(bf16[64,2048]{1,0:T(8,128)(2,1)} %q.1, bf16[1024,128]{1,0:T(8,128)(2,1)} %ck.1, bf16[1024,128]{1,0:T(8,128)(2,1)} %cv.1, bf16[64,128]{1,0:T(8,128)(2,1)} %nk.1, bf16[64,128]{1,0:T(8,128)(2,1)} %nv.1), custom_call_target="tpu_custom_call" | custom-call | tf_op jit(solution)/shard_map/gather/pallas_call | solution.py:279
  67.7 0.0 copy-start.1
  67.7 1.6 copy-done.1
  69.3 0.0 copy-start.2
  69.3 0.7 copy-done.2
  70.0 0.0 copy-start.3
  70.0 0.7 copy-done.3
  70.7 0.0 copy-start.4
  70.7 0.7 copy-done.4
  71.3 0.0 copy-start
  71.3 35.4 %attention.1 = (bf16[8,64,2048]{2,1,0:T(8,128)(2,1)S(1)}, f32[8,64,128]{2,1,0:T(8,128)S(1)}) custom-call(s32[256]{0:T(256)S(1)} %copy-done.2, s32[16]{0:T(128)S(1)} %copy-done.3, s32[32]{0:T(128)S(1)} %copy-done.4, s32[1]{0:T(128)} %bitcast.place, bf16[8,64,2048]{2,1,0:T(8,128)(2,1)S(1)} %copy-done.1, bf16[8704,128]{1,0:T(8,128)(2,1)} %bitcast.2), custom_call_target="tpu_custom_call" | custom-call | tf_op jit(solution)/shard_map/attention/pallas_call | solution.py:163
  106.7 0.0 collective-permute-done.wp
  106.7 0.0 copy-start.5
  106.7 1.3 copy-done.5
  108.0 0.0 copy-done
  108.0 74.5 %project.1 = bf16[512,512]{1,0:T(8,128)(2,1)S(1)} custom-call(bf16[8,64,2048]{2,1,0:T(8,128)(2,1)S(1)} %get-tuple-element.11.o, f32[8,64,128]{2,1,0:T(8,128)S(1)} %get-tuple-element.12.st, bf16[2048,512]{1,0:T(8,128)(2,1)S(1)} %copy-done, bf16[2048,512]{1,0:T(8,128)(2,1)} %copy-done.5), custom_call_target="tpu_custom_call" | custom-call | tf_op jit(solution)/shard_map/project/pallas_call | solution.py:448
  182.6 0.8 copy.11
Async XLA Ops:
  0.0 106.7 %collective-permute-start = (bf16[2048,512]{1,0:T(8,128)(2,1)}, bf16[2048,512]{1,0:T(8,128)(2,1)S(1)}, u32[]{:S(2)}, u32[]{:S(2)}) collective-permute-start(bf16[2048,512]{1,0:T(8,128)(2,1)} %w.1), channel_id=1, source_target_pairs={{0,64},{4,68},{8,72},{12,76},{16,80},{20,84},{24,88},{28,92},{32,9... | collective-permute-start | bytes 6291464 | tf_op jit(solution)/shard_map/ppermute | solution.py:467
  67.7 1.6 copy-start.1
  69.3 0.7 copy-start.2
  70.0 0.7 copy-start.3
  70.7 0.7 copy-start.4
  71.3 36.7 %copy-start = (bf16[2048,512]{1,0:T(8,128)(2,1)S(1)}, bf16[2048,512]{1,0:T(8,128)(2,1)}, u32[]{:S(2)}) copy-start(bf16[2048,512]{1,0:T(8,128)(2,1)} %w.1) | copy-start | bytes 6291460
  106.7 1.3 copy-start.5

commit v2 on v1

v2 whole, which is shorter than its diff:
```python
import functools
import jax, jax.numpy as jnp
from jax import lax
from jax.experimental import pallas as pl
from jax.experimental.pallas import tpu as pltpu
from jax.sharding import PartitionSpec as P

HD=128; BLK=128; NEG=-1e30
SCALE=HD**-0.5
L2E=1.4426950408889634
ROWS=64; HEADS=16; CR=1024; HALF=CR+ROWS; MEM=2*HALF
SUB=1024

def attn_kernel(cdocs, ndocs, tiles, place, q_hbm, kv_hbm, o_hbm, st_hbm, q_ref, kv_ref, o_ref, st_ref,
                q_s, m_s, l_s, acc_s, lst, sems, *, nb):
    q_in = lambda g: pltpu.make_async_copy(q_hbm.at[g], q_ref.at[g], sems.at[0, g])
    o_out = lambda g: pltpu.make_async_copy(o_ref.at[g], o_hbm.at[g], sems.at[1, g])
    kv_in = pltpu.make_async_copy(kv_hbm, kv_ref, sems.at[2, 0])
    st_out = pltpu.make_async_copy(st_ref, st_hbm, sems.at[2, 1])
    kv_in.start()
    for g in range(8):
        q_in(g).start()
    kv_in.wait()

    def run(g, _):
        q_in(g).wait()
        attend_run(g, cdocs, ndocs, tiles, place, q_ref, kv_ref, o_ref, st_ref, q_s, m_s, l_s, acc_s, lst, nb)
        o_out(g).start()
        return 0
    lax.fori_loop(0, 8, run, 0)
    st_out.start()
    for g in range(8):
        o_out(g).wait()
    st_out.wait()


def attend_run(g, cdocs, ndocs, tiles, place, q_ref, kv_ref, o_ref, st_ref, q_s, m_s, l_s, acc_s, lst, nb):
    c = place[0]
    y = c % 4
    src = g * 4 + y
    members = [c - y + i for i in range(4)]
    tq = tiles[src]
    qd = ndocs[tq // 2]
    nrow = ROWS*HEADS
    for h in range(HEADS):
        q_s[h*ROWS:(h+1)*ROWS, :] = q_ref[g, :, h*HD:(h+1)*HD]
    m_s[...] = jnp.full_like(m_s, NEG)
    l_s[...] = jnp.zeros_like(l_s)
    acc_s[...] = jnp.zeros_like(acc_s)
    n = jnp.int32(0)
    for mi, c in enumerate(members):
        def add(b, n):
            ok = cdocs[c*8 + b] == qd
            lst[n] = mi*MEM + b*BLK
            return n + ok.astype(jnp.int32)
        n = lax.fori_loop(0, 8, add, n)

    def slow_step(kc, vc, mask_fn):
        for t in range(nrow//SUB):
            r = pl.ds(t*SUB, SUB)
            s = lax.dot_general(q_s[r, :], kc, (((1,),(1,)),((),())), preferred_element_type=jnp.float32)
            if mask_fn is not None:
                s = mask_fn(s)
            w = s.shape[1]//128
            mx = s[:, :128]
            for i in range(1, w):
                mx = jnp.maximum(mx, s[:, i*128:(i+1)*128])
            mx = jnp.max(mx, axis=1, keepdims=True)
            m_old = m_s[r, :]
            m_new = jnp.maximum(m_old, mx)
            alpha = jnp.exp2((m_old - m_new)*(SCALE*L2E))
            p = [jnp.exp2((s[:, i*128:(i+1)*128] - m_new)*(SCALE*L2E)) for i in range(w)]
            ps = p[0]
            for i in range(1, w):
                ps = ps + p[i]
            l_s[r, :] = l_s[r, :]*alpha + ps
            m_s[r, :] = m_new
            pb = jnp.concatenate([x.astype(jnp.bfloat16) for x in p], axis=1)
            acc_s[r, :] = acc_s[r, :]*alpha + jnp.dot(pb, vc, preferred_element_type=jnp.float32)


    def peak(kc, mask_fn):
        for t in range(nrow//SUB):
            r = pl.ds(t*SUB, SUB)
            s = lax.dot_general(q_s[r, :], kc, (((1,),(1,)),((),())), preferred_element_type=jnp.float32)
            if mask_fn is not None:
                s = mask_fn(s)
            w = s.shape[1]//128
            mx = s[:, :128]
            for i in range(1, w):
                mx = jnp.maximum(mx, s[:, i*128:(i+1)*128])
            m_s[r, :] = jnp.broadcast_to(jnp.max(mx, axis=1, keepdims=True), (SUB, 128))

    def step(kc, vc, mask_fn):
        for t in range(nrow//SUB):
            r = pl.ds(t*SUB, SUB)
            s = lax.dot_general(q_s[r, :], kc, (((1,),(1,)),((),())), preferred_element_type=jnp.float32)
            if mask_fn is not None:
                s = mask_fn(s)
            w = s.shape[1]//128
            m = m_s[r, :]
            p = [jnp.exp2((s[:, i*128:(i+1)*128] - m)*(SCALE*L2E)) for i in range(w)]
            ps = p[0]
            for i in range(1, w):
                ps = ps + p[i]
            l_s[r, :] = l_s[r, :] + ps
            pb = jnp.concatenate([x.astype(jnp.bfloat16) for x in p], axis=1)
            acc_s[r, :] = acc_s[r, :] + jnp.dot(pb, vc, preferred_element_type=jnp.float32)

    def at(off, rows=BLK):
        return kv_ref[pl.ds(pl.multiple_of(off, 64), rows), :]

    def chunks(step):
        def chunk(base, size):
            offs = [lst[base + j] for j in range(size)]
            kc = jnp.concatenate([at(o) for o in offs], axis=0)
            vc = jnp.concatenate([at(o + HALF) for o in offs], axis=0)
            step(kc, vc, None)
        def body(i, _):
            chunk(i*nb, nb)
            return 0
        lax.fori_loop(0, n // nb, body, 0)
        size = nb // 2
        while size >= 1:
            @pl.when((n // size) % 2 == 1)
            def _(size=size):
                chunk((n // (2*size))*(2*size), size)
            size //= 2
    kcs = []; vcs = []
    newlims = []
    for mi, c in enumerate(members):
        tk = tiles[c]
        same_doc = ndocs[tk // 2] == qd
        full_ok = same_doc & (tk < tq)
        diag = tk == tq
        newlims.append((jnp.where(full_ok, 1 << 20, jnp.where(diag, 0, -1)), jnp.where(diag, 1, 0)))
        kcs.append(kv_ref[mi*MEM + CR: mi*MEM + HALF, :])
        vcs.append(kv_ref[mi*MEM + HALF + CR: (mi+1)*MEM, :])
    kc = jnp.concatenate(kcs, axis=0); vc = jnp.concatenate(vcs, axis=0)
    any_new = functools.reduce(jnp.logical_or, [lim >= 0 for lim, _ in newlims])
    def mask(s):
        row = lax.broadcasted_iota(jnp.int32, (SUB, 128), 0) % ROWS
        lane = lax.broadcasted_iota(jnp.int32, (SUB, 128), 1)
        out = []
        for a in range(2):
            (b0, d0), (b1, d1) = newlims[2*a], newlims[2*a+1]
            lo = row*d0 + b0
            hi = row*d1 + b1
            ok = lane <= jnp.where(lane < ROWS, lo, hi + ROWS)
            k0 = a*128
            out.append(jnp.where(ok, s[:, k0:k0+128], NEG))
        return jnp.concatenate(out, axis=1)
    @pl.when(n > 0)
    def _():
        peak(at(lst[0]), None)
    @pl.when((n == 0) & any_new)
    def _():
        peak(kc, mask)
    chunks(step)
    @pl.when(any_new)
    def _():
        step(kc, vc, mask)
    @pl.when(jnp.logical_not(jnp.max(l_s[...]) < 1e30))
    def _():
        m_s[...] = jnp.full_like(m_s, NEG)
        l_s[...] = jnp.zeros_like(l_s)
        acc_s[...] = jnp.zeros_like(acc_s)
        chunks(slow_step)
        @pl.when(any_new)
        def _():
            slow_step(kc, vc, mask)
    lane = lax.broadcasted_iota(jnp.int32, (ROWS, 128), 1)
    st = jnp.full((ROWS, 128), NEG, jnp.float32)
    for h in range(HEADS):
        r = pl.ds(h*ROWS, ROWS)
        l = jnp.sum(l_s[r, :], axis=1, keepdims=True)
        l = jnp.maximum(l, 1e-30)
        o_ref[g, :, h*HD:(h+1)*HD] = (acc_s[r, :] / l).astype(jnp.bfloat16)
        lse = m_s[r, :]*SCALE + jnp.log(l)
        st = jnp.where(lane == h, lse, st)
    st_ref[g] = st

def attention(qg, kvg, cdocs, ndocs, tiles, place, nb=4):
    nrow = ROWS*HEADS
    smem, anywhere = pl.BlockSpec(memory_space=pltpu.SMEM), pl.BlockSpec(memory_space=pl.ANY)
    return pl.pallas_call(
        functools.partial(attn_kernel, nb=nb),
        in_specs=[smem] * 4 + [anywhere] * 2,
        out_specs=[anywhere] * 2,
        scratch_shapes=[pltpu.VMEM((8, ROWS, HEADS*HD), jnp.bfloat16), pltpu.VMEM((4*MEM, HD), jnp.bfloat16),
                        pltpu.VMEM((8, ROWS, HEADS*HD), jnp.bfloat16), pltpu.VMEM((8, ROWS, 128), jnp.float32),
                        pltpu.VMEM((nrow, HD), jnp.bfloat16), pltpu.VMEM((nrow, 128), jnp.float32),
                        pltpu.VMEM((nrow, 128), jnp.float32), pltpu.VMEM((nrow, HD), jnp.float32),
                        pltpu.SMEM((40,), jnp.int32), pltpu.SemaphoreType.DMA((3, 8))],
        out_shape=[jax.ShapeDtypeStruct((8, ROWS, HEADS*HD), jnp.bfloat16),
                   jax.ShapeDtypeStruct((8, ROWS, 128), jnp.float32)],
        compiler_params=pltpu.CompilerParams(vmem_limit_bytes=56 << 20),
        name="attention",
    )(cdocs, ndocs, tiles, place, qg, kvg)


MESH = pl.DeviceIdType.MESH
WROWS = 768


def coords():
    c = lax.axis_index("ctx")
    return c // 16, (c // 4) % 4, c % 4


def ctx_of(z, x, y):
    return z * 16 + x * 4 + y


def send(src, dst, sems, i, device):
    copy = pltpu.make_async_remote_copy(
        src_ref=src, dst_ref=dst, send_sem=sems[0].at[i], recv_sem=sems[1].at[i],
        device_id=device, device_id_type=MESH)
    copy.start()
    return copy


def arrive(ref, sems, i, device):
    pltpu.make_async_remote_copy(
        src_ref=ref, dst_ref=ref, send_sem=sems[0].at[i], recv_sem=sems[1].at[i],
        device_id=device, device_id_type=MESH).wait_recv()


def greet(peers):
    barrier = pltpu.get_barrier_semaphore()
    for device in peers:
        pl.semaphore_signal(barrier, inc=1, device_id=device, device_id_type=MESH)
    pl.semaphore_wait(barrier, len(peers))


def gather_kernel(q, ck, cv, nk, nv, w, q_out, kv_out, w_out, rest_out, qg, kvg, wg, wr, ws, ssem, rsem, lsem, osem):
    z, x, y = coords()
    sems = (ssem, rsem)
    zp = 1 - z
    xr, xl, yr, yl = (x + 1) % 4, (x + 3) % 4, (y + 1) % 4, (y + 3) % 4
    x2, y2 = (x + 2) % 4, (y + 2) % 4
    dev = lambda z, x, y: {"ctx": ctx_of(z, x, y)}
    to_yr, to_yl, to_xr, to_xl, to_z = dev(z, x, yr), dev(z, x, yl), dev(z, xr, y), dev(z, xl, y), dev(zp, x, y)
    slot = lambda z, x: z * 4 + x
    me = slot(z, x)
    out = []
    pieces = [(ck, 0, CR), (nk, CR, ROWS), (cv, HALF, CR), (nv, HALF + CR, ROWS)]
    locs = [pltpu.make_async_copy(q, qg.at[me], lsem.at[0])]
    for i, (src, off, n) in enumerate(pieces):
        locs.append(pltpu.make_async_copy(src, kvg.at[y, pl.ds(off, n)], lsem.at[1 + i]))
    locs.append(pltpu.make_async_copy(w.at[pl.ds(0, WROWS)], ws, lsem.at[5]))
    locs.append(pltpu.make_async_copy(w.at[pl.ds(WROWS, 2048 - WROWS)], wr, lsem.at[6]))
    for cp in locs:
        cp.start()
    greet([to_yr, to_yl, to_xr, to_xl, to_z])
    kh, vh = pl.ds(0, HALF), pl.ds(HALF, HALF)
    saves = []

    def save(src, dst):
        saves.append(pltpu.make_async_copy(src, dst, osem.at[len(saves)]))
        saves[-1].start()

    locs[0].wait()
    out.append(send(qg.at[me], qg.at[me], sems, 0, to_z))
    out.append(send(qg.at[me], qg.at[me], sems, 9, to_xr))
    out.append(send(qg.at[me], qg.at[me], sems, 10, to_xl))
    for cp in locs[1:5]:
        cp.wait()
    out.append(send(kvg.at[y, kh], kvg.at[y, kh], sems, 1, to_yr))
    out.append(send(kvg.at[y, vh], kvg.at[y, vh], sems, 2, to_yl))
    out.append(send(kvg.at[y, vh], kvg.at[y, vh], sems, 3, to_yr))
    out.append(send(kvg.at[y, kh], kvg.at[y, kh], sems, 4, to_yl))
    locs[5].wait()
    out.append(send(ws, wg, sems, 19, to_z))
    save(qg.at[me], q_out.at[me])
    save(kvg.at[y], kv_out.at[y])
    locs[6].wait()
    save(wr, rest_out)
    other = slot(zp, x)
    arrive(qg.at[other], sems, 0, to_z)
    out.append(send(qg.at[other], qg.at[other], sems, 11, to_xr))
    out.append(send(qg.at[other], qg.at[other], sems, 12, to_xl))
    save(qg.at[other], q_out.at[other])
    lo, hi = pl.ds(0, 32), pl.ds(32, 32)
    arrive(qg.at[slot(z, xl)], sems, 9, to_xl)
    out.append(send(qg.at[slot(z, xl), lo], qg.at[slot(z, xl), lo], sems, 13, to_xr))
    save(qg.at[slot(z, xl)], q_out.at[slot(z, xl)])
    arrive(qg.at[slot(z, xr)], sems, 10, to_xr)
    out.append(send(qg.at[slot(z, xr), hi], qg.at[slot(z, xr), hi], sems, 14, to_xl))
    save(qg.at[slot(z, xr)], q_out.at[slot(z, xr)])
    arrive(kvg.at[yl, kh], sems, 1, to_yl)
    out.append(send(kvg.at[yl, kh], kvg.at[yl, kh], sems, 17, to_yr))
    arrive(kvg.at[yr, vh], sems, 2, to_yr)
    out.append(send(kvg.at[yr, vh], kvg.at[yr, vh], sems, 18, to_yl))
    arrive(qg.at[slot(zp, xl)], sems, 11, to_xl)
    out.append(send(qg.at[slot(zp, xl), lo], qg.at[slot(zp, xl), lo], sems, 15, to_xr))
    save(qg.at[slot(zp, xl)], q_out.at[slot(zp, xl)])
    arrive(qg.at[slot(zp, xr)], sems, 12, to_xr)
    out.append(send(qg.at[slot(zp, xr), hi], qg.at[slot(zp, xr), hi], sems, 16, to_xl))
    save(qg.at[slot(zp, xr)], q_out.at[slot(zp, xr)])
    arrive(kvg.at[yl, vh], sems, 3, to_yl)
    arrive(kvg.at[yr, kh], sems, 4, to_yr)
    save(kvg.at[yl], kv_out.at[yl])
    save(kvg.at[yr], kv_out.at[yr])
    arrive(qg.at[slot(z, x2), lo], sems, 13, to_xl)
    arrive(qg.at[slot(z, x2), hi], sems, 14, to_xr)
    save(qg.at[slot(z, x2)], q_out.at[slot(z, x2)])
    arrive(qg.at[slot(zp, x2), lo], sems, 15, to_xl)
    arrive(qg.at[slot(zp, x2), hi], sems, 16, to_xr)
    save(qg.at[slot(zp, x2)], q_out.at[slot(zp, x2)])
    arrive(kvg.at[y2, kh], sems, 17, to_yl)
    arrive(kvg.at[y2, vh], sems, 18, to_yr)
    save(kvg.at[y2], kv_out.at[y2])
    arrive(wg, sems, 19, to_z)
    save(wg, w_out)
    for cp in saves:
        cp.wait()
    for cp in out:
        cp.wait_send()


def gather(q, ck, cv, nk, nv, w):
    hbm, bf = pl.BlockSpec(memory_space=pl.ANY), jnp.bfloat16
    return pl.pallas_call(
        gather_kernel,
        in_specs=[hbm] * 6,
        out_specs=[hbm] * 4,
        out_shape=[jax.ShapeDtypeStruct((8, ROWS, HEADS * HD), jnp.bfloat16),
                   jax.ShapeDtypeStruct((4, MEM, HD), jnp.bfloat16),
                   jax.ShapeDtypeStruct((WROWS, 512), jnp.bfloat16),
                   jax.ShapeDtypeStruct((2048 - WROWS, 512), jnp.bfloat16)],
        scratch_shapes=[pltpu.VMEM((8, ROWS, HEADS * HD), bf), pltpu.VMEM((4, MEM, HD), bf), pltpu.VMEM((WROWS, 512), bf),
                        pltpu.VMEM((2048 - WROWS, 512), bf), pltpu.VMEM((WROWS, 512), bf), pltpu.SemaphoreType.DMA((20,)),
                        pltpu.SemaphoreType.DMA((20,)), pltpu.SemaphoreType.DMA((7,)), pltpu.SemaphoreType.DMA((14,))],
        compiler_params=pltpu.CompilerParams(collective_id=0, has_side_effects=True, vmem_limit_bytes=56 << 20),
        name="gather",
    )(q, ck, cv, nk, nv, w)


def merge(parts, stats):
    largest = functools.reduce(jnp.maximum, stats)
    e = [jnp.exp(s - largest) for s in stats]
    total = functools.reduce(jnp.add, e)
    inverse = 1.0 / total
    e = [a * inverse for a in e]
    cols = []
    for head in range(HEADS):
        a = None
        for weight, part in zip(e, parts):
            term = weight[:, head:head + 1] * part[:, head * HD:(head + 1) * HD].astype(jnp.float32)
            a = term if a is None else a + term
        cols.append(a.astype(jnp.bfloat16))
    return cols, largest + jnp.log(total)


def put(ref, cols):
    for head, a in enumerate(cols):
        ref[:, head * HD:(head + 1) * HD] = a


def project_kernel(o_hbm, st_hbm, w, wlo, whi, out, o, st, px, sx, pz, sz, mz, nz, rz, tz, mx, nx, rx, tx_s, attg, w_s, ct, cr, acc, zt, zr,
                   a_s, a_r, b_s, b_r, c_s, c_r, d_s, d_r, gs, gr, cs, crs, zs, zrs, lsem):
    z, x, y = coords()
    t = lax.axis_index("tp")
    h, k = t // 2, t % 2
    dev = lambda z, x, y: {"ctx": ctx_of(z, x, y)}
    zdev = lambda b, zh: {"ctx": ctx_of(b, x, y), "tp": zh * 2 + k}
    zp = 1 - z
    xr, xl, yr, yl = (x + 1) % 4, (x + 3) % 4, (y + 1) % 4, (y + 3) % 4
    core = {"tp": h * 2 + 1 - k}
    to_yr, to_yl, to_xr, to_xl = dev(z, x, yr), dev(z, x, yl), dev(z, xr, y), dev(z, xl, y)
    to_z = dev(zp, x, y)
    to_x = lambda d: dev(z, (x + d) % 4, y)
    ready = [pltpu.make_async_copy(o_hbm, o, lsem.at[3]), pltpu.make_async_copy(st_hbm, st, lsem.at[4])]
    for cp in ready:
        cp.start()
    greet([to_xr, to_xl, to_x(2), to_z, to_yr, to_yl, core, zdev(0, 1 - h), zdev(1, 1 - h)])
    lo, hi = pl.ds(0, 32), pl.ds(32, 32)
    outs = []

    for cp in ready:
        cp.wait()
    for d in (2, 1, 3, 0):
        xx = (x + d) % 4
        outs.append(send(st.at[zp, xx, hi], sz.at[xx], (b_s.at[1], b_r.at[1]), d, to_z))
        outs.append(send(o.at[zp, xx, hi], pz.at[xx], (b_s.at[0], b_r.at[0]), d, to_z))
    for d in (2, 1, 3):
        xx = (x + d) % 4
        outs.append(send(st.at[:, xx, lo], sx.at[x], (a_s.at[1], a_r.at[1]), d, to_x(d)))
        outs.append(send(o.at[:, xx, lo], px.at[x], (a_s.at[0], a_r.at[0]), d, to_x(d)))
    weights = [pltpu.make_async_copy(w, w_s.at[z], lsem.at[0]),
               pltpu.make_async_copy(wlo, w_s.at[zp, pl.ds(0, WROWS)], lsem.at[1]),
               pltpu.make_async_copy(whi, w_s.at[zp, pl.ds(WROWS, 2048 - WROWS)], lsem.at[2])]
    for cp in weights:
        cp.start()
    for d in (2, 1, 3, 0):
        xx = (x + d) % 4
        arrive(sz.at[xx], (b_s.at[1], b_r.at[1]), d, to_z)
        arrive(pz.at[xx], (b_s.at[0], b_r.at[0]), d, to_z)
        cols, lse = merge([o[z, xx, 32:64, :], pz[xx]], [st[z, xx, 32:64, :], sz[xx]])
        if d == 0:
            put(rx.at[x], cols)
            tx_s[x] = lse
        else:
            put(mx.at[d - 1], cols)
            nx[d - 1] = lse
            outs.append(send(nx.at[d - 1], tx_s.at[x], (d_s.at[1], d_r.at[1]), d, to_x(d)))
            outs.append(send(mx.at[d - 1], rx.at[x], (d_s.at[0], d_r.at[0]), d, to_x(d)))
    for d in (2, 1, 3):
        xx = (x + 4 - d) % 4
        arrive(sx.at[xx], (a_s.at[1], a_r.at[1]), d, to_x(4 - d))
        arrive(px.at[xx], (a_s.at[0], a_r.at[0]), d, to_x(4 - d))
    others = [(x + d) % 4 for d in (1, 2, 3)]
    cols, lse = merge([o[zp, x, 0:32, :]] + [px[xx, zp] for xx in others],
                      [st[zp, x, 0:32, :]] + [sx[xx, zp] for xx in others])
    put(mz, cols)
    nz[...] = lse
    outs.append(send(nz, tz, (c_s, c_r), 1, to_z))
    outs.append(send(mz, rz, (c_s, c_r), 0, to_z))
    own_cols, own_lse = merge([o[z, x, 0:32, :]] + [px[xx, z] for xx in others],
                              [st[z, x, 0:32, :]] + [sx[xx, z] for xx in others])
    mine = x * 4 + y
    put(attg.at[mine, lo], own_cols)
    arrive(tz, (c_s, c_r), 1, to_z)
    arrive(rz, (c_s, c_r), 0, to_z)
    cols, _ = merge([attg[mine, 0:32, :], rz[...]], [own_lse, tz[...]])
    put(attg.at[mine, lo], cols)

    slot = lambda x, y: x * 4 + y

    def block(hf, a, b, part=None):
        s = slot((x + a) % 4, (y + b) % 4) if hf == 0 else slot((x + b) % 4, (y + a) % 4)
        return attg.at[s, pl.ds(32 * hf, 32) if part is None else pl.ds(32 * hf + 16 * part, 16)]

    def ways(hf, stage):
        return (to_xr, to_xl) if (hf == 0) == (stage == 0) else (to_yr, to_yl)

    def both(hf, stage, a, i):
        right, left = ways(hf, stage)
        ref = block(hf, a, 0)
        outs.append(send(ref, ref, (gs.at[hf], gr.at[hf]), i, right))
        outs.append(send(ref, ref, (gs.at[hf], gr.at[hf]), i + 1, left))

    def at(stage, a, n):
        return (n, 0) if stage == 0 else (a, n)

    def relay(hf, stage, a, i):
        right, left = ways(hf, stage)
        arrive(block(hf, *at(stage, a, 3)), (gs.at[hf], gr.at[hf]), i, left)
        ref = block(hf, *at(stage, a, 3), part=0)
        outs.append(send(ref, ref, (gs.at[hf], gr.at[hf]), i + 2, right))
        arrive(block(hf, *at(stage, a, 1)), (gs.at[hf], gr.at[hf]), i + 1, right)
        ref = block(hf, *at(stage, a, 1), part=1)
        outs.append(send(ref, ref, (gs.at[hf], gr.at[hf]), i + 3, left))

    def last(hf, stage, a, i):
        right, left = ways(hf, stage)
        arrive(block(hf, *at(stage, a, 2), part=0), (gs.at[hf], gr.at[hf]), i + 2, left)
        arrive(block(hf, *at(stage, a, 2), part=1), (gs.at[hf], gr.at[hf]), i + 3, right)

    both(0, 0, 0, 0)
    both(0, 1, 0, 4)
    for d in (2, 1, 3):
        xx = (x + 4 - d) % 4
        arrive(tx_s.at[xx], (d_s.at[1], d_r.at[1]), d, to_x(4 - d))
        arrive(rx.at[xx], (d_s.at[0], d_r.at[0]), d, to_x(4 - d))
    cols, _ = merge([rx[i] for i in range(4)], [tx_s[i] for i in range(4)])
    put(attg.at[mine, hi], cols)
    both(1, 0, 0, 0)
    both(1, 1, 0, 4)
    for hf in (0, 1):
        relay(hf, 0, 0, 0)
        both(hf, 1, 3, 8)
        both(hf, 1, 1, 12)
    for hf in (0, 1):
        last(hf, 0, 0, 0)
        both(hf, 1, 2, 16)
    for a, i in ((0, 4), (3, 8), (1, 12), (2, 16)):
        for hf in (0, 1):
            relay(hf, 1, a, i)
    for cp in weights:
        cp.wait()

    def places(p):
        hf, late = p % 2, p // 2
        if hf == 0:
            first = [(2 * (1 - k) + i, (y + n) % 4) for i in (0, 1) for n in ((1, 3), (0, 2))[late]]
            then = [(2 * k + i, (y + n) % 4) for i in (0, 1) for n in ((1, 3), (0, 2))[late]]
        else:
            parity = (x + 1 - late) % 2
            first = [(2 * (1 - k) + parity, n) for n in range(4)]
            then = [(2 * k + parity, n) for n in range(4)]
        return hf, first, then

    mine_at = lambda b: (h == z) & (b == z)

    def multiply(p):
        hf, first, then = places(p)
        lhs = jnp.concatenate([attg[slot(*s), 32 * hf:32 * hf + 32, :] for s in first + then], axis=0)
        for b in (0, 1):
            r = jnp.dot(lhs, w_s[b], preferred_element_type=jnp.float32)
            ct[p, b] = r[:128].astype(jnp.bfloat16)
            acc[p, b] = r[128:]
        outs.append(send(ct.at[p], cr.at[p], (cs, crs), p, core))

    def exchange(p):
        arrive(cr.at[p], (cs, crs), p, core)
        for b in (0, 1):
            zt[p, b] = (acc[p, b] + cr[p, b].astype(jnp.float32)).astype(jnp.bfloat16)

            @pl.when(jnp.logical_not(mine_at(b)))
            def _():
                send(zt.at[p, b], zr.at[h, p], (zs, zrs.at[h]), p * 2 + b, zdev(b, z))

            @pl.when(mine_at(b))
            def _():
                zr[h, p] = zt[p, b]

    multiply(0)
    multiply(1)
    exchange(0)
    exchange(1)
    for a, i in ((0, 4), (3, 8), (1, 12), (2, 16)):
        for hf in (0, 1):
            last(hf, 1, a, i)
    multiply(2)
    multiply(3)
    exchange(2)
    exchange(3)
    for p in range(4):
        for s in (0, 1):
            @pl.when(jnp.logical_not((s == h) & (z == h)))
            def _():
                pltpu.make_async_remote_copy(
                    src_ref=zr.at[s, p], dst_ref=zr.at[s, p], send_sem=zs.at[0], recv_sem=zrs.at[s, p * 2 + z],
                    device_id=zdev(h, s), device_id_type=MESH).wait_recv()
        total = (zr[0, p].astype(jnp.float32) + zr[1, p].astype(jnp.float32)).astype(jnp.bfloat16)
        hf, _, then = places(p)
        for i, (xx, yy) in enumerate(then):
            off = (slot(xx, yy) - 8 * k) * 64 + 32 * hf
            out[pl.ds(pl.multiple_of(off, 32), 32), :] = total[32 * i:32 * i + 32]
    for p in range(4):
        for b in (0, 1):
            @pl.when(jnp.logical_not(mine_at(b)))
            def _():
                pltpu.make_async_remote_copy(
                    src_ref=zt.at[p, b], dst_ref=zt.at[p, b], send_sem=zs.at[p * 2 + b], recv_sem=zrs.at[0, 0],
                    device_id=zdev(b, z), device_id_type=MESH).wait_send()
    for cp in outs:
        cp.wait_send()


def project(o, st, w, wlo, whi):
    hbm, vmem = pl.BlockSpec(memory_space=pl.ANY), pl.BlockSpec(memory_space=pltpu.VMEM)
    dma = pltpu.SemaphoreType.DMA
    bf, f32 = jnp.bfloat16, jnp.float32
    wide = HEADS * HD
    return pl.pallas_call(
        project_kernel,
        in_specs=[hbm] * 5,
        out_specs=vmem,
        out_shape=jax.ShapeDtypeStruct((512, 512), bf),
        scratch_shapes=[
            pltpu.VMEM((2, 4, ROWS, wide), bf), pltpu.VMEM((2, 4, ROWS, 128), f32),
            pltpu.VMEM((4, 2, 32, wide), bf), pltpu.VMEM((4, 2, 32, 128), f32),
            pltpu.VMEM((4, 32, wide), bf), pltpu.VMEM((4, 32, 128), f32),
            pltpu.VMEM((32, wide), bf), pltpu.VMEM((32, 128), f32),
            pltpu.VMEM((32, wide), bf), pltpu.VMEM((32, 128), f32),
            pltpu.VMEM((3, 32, wide), bf), pltpu.VMEM((3, 32, 128), f32),
            pltpu.VMEM((4, 32, wide), bf), pltpu.VMEM((4, 32, 128), f32),
            pltpu.VMEM((16, ROWS, wide), bf), pltpu.VMEM((2, 2048, 512), bf),
            pltpu.VMEM((4, 2, 128, 512), bf), pltpu.VMEM((4, 2, 128, 512), bf), pltpu.VMEM((4, 2, 128, 512), f32),
            pltpu.VMEM((4, 2, 128, 512), bf), pltpu.VMEM((2, 4, 128, 512), bf),
            dma((2, 4)), dma((2, 4)), dma((2, 4)), dma((2, 4)), dma((2,)), dma((2,)), dma((2, 4)), dma((2, 4)),
            dma((2, 20)), dma((2, 20)), dma((4,)), dma((4,)), dma((8,)), dma((2, 8)), dma((5,)),
        ],
        compiler_params=pltpu.CompilerParams(collective_id=1, has_side_effects=True, vmem_limit_bytes=56 << 20),
        name="project",
    )(o, st, w, wlo, whi)


def shards(new_queries, new_keys, new_values, cache_keys, cache_values, out_weight, cache_docs, new_docs, slot_tile):
    qg, kvg, wlo, rest = gather(new_queries, cache_keys, cache_values, new_keys, new_values, out_weight)
    whi = lax.ppermute(rest, "ctx", [(i, i ^ 16) for i in range(32)])
    place = jnp.reshape(lax.axis_index("ctx"), (1,)).astype(jnp.int32)
    o, st = attention(qg, kvg.reshape(4 * MEM, HD), cache_docs, new_docs, slot_tile, place)
    return project(o.reshape(2, 4, ROWS, HEADS * HD), st.reshape(2, 4, ROWS, 128), out_weight, wlo, whi)


def solution(mesh):
    return jax.shard_map(
        shards,
        mesh=mesh,
        in_specs=(
            P("ctx", "tp"),
            P("ctx", "tp"),
            P("ctx", "tp"),
            P("ctx", "tp"),
            P("ctx", "tp"),
            P("tp", "ctx"),
            P(),
            P(),
            P(),
        ),
        out_specs=P("tp", "ctx"),
        check_vma=False,
    )
```

time: 184 us -> 131 us (0.71)
  Pallas kernels: 175 us -> 127 us
  local copies, waits for them, and re-layouts: 5.71 us -> 2.93 us
  starting transfers between devices: 2.47 us -> 0.09 us
    pallas_call x3, Pallas kernels: 175 us -> 127 us  [the longest x1 69.9 us: project(): pl.pallas_call(project_kernel, in_specs=[hbm] * 5, out_specs=vmem, out_sh...]
    unnamed x13 -> x3, local copies, waits for them, and re-layouts: 5.71 us -> 2.93 us
    ppermute x1, starting transfers between devices: 2.47 us -> 0.09 us  [shards(): whi = lax.ppermute(rest, 'ctx', [(i, i ^ 16) for i in range(32)])]
  transfers between devices with their start and end apart: 1 -> 1, of which waited for: 0 -> 1; matrix products, arithmetic and copies ran while one was open for 0% -> 0% of each run, Pallas kernels for 55% -> 21%
where the time goes in v2:
time: 131 us
  Pallas kernels  127 us (97%)
  local copies, waits for them, and re-layouts  2.93 us (2%)
    pallas_call x1, Pallas kernels, project(): pl.pallas_call(project_kernel, in_specs=[hbm] * 5, out_specs=vmem, out_sh...  69.9 us
    pallas_call x1, Pallas kernels, gather(): pl.pallas_call(gather_kernel, in_specs=[hbm] * 6, out_specs=[hbm] * 4, ou...  29.3 us
    pallas_call x1, Pallas kernels, attention(): pl.pallas_call(functools.partial(attn_kernel, nb=nb), in_specs=[smem] * 4...  27.6 us
    unnamed x3, local copies, waits for them, and re-layouts  2.93 us
  transfers between devices with their start and end apart: 1, of which 1 were waited for; matrix products, arithmetic and copies ran while one was open for 0% of the time, Pallas kernels for 21%

profile of v2, /device:TPU:1, one launch (start us, length us, event | category | flops | bytes accessed | tf_op | source)
XLA Modules:
  0.0 131.2 jit_solution(6545483616996278677)
XLA Ops:
  0.0 29.3 %gather.1 = (bf16[8,64,2048]{2,1,0:T(8,128)(2,1)}, bf16[4,2176,128]{2,1,0:T(8,128)(2,1)}, bf16[768,512]{1,0:T(8,128)(2,1)}, bf16[1280,512]{1,0:T(8,128)(2,1)}) custom-call(bf16[64,2048]{1,0:T(8,128)(2,1)} %q.1, bf16[1024,128]{1,0:T(8,128)(2,1)} %ck.1, bf16[1024,128]{1,0:T(8,128)(2,1)} %cv.1, bf16[64,128]{1,0:T(8,128)(2,1)} %nk.1, bf16[64,128]{1,0:T(8,128)(2,1)} %nv.1, ...), custom_call_target="tpu_custom_call" | custom-call | tf_op jit(solution)/shard_map/gather/pallas_call | solution.py:324
  29.3 0.1 collective-permute-start
  29.4 27.6 %attention.1 = (bf16[8,64,2048]{2,1,0:T(8,128)(2,1)}, f32[8,64,128]{2,1,0:T(8,128)}) custom-call(s32[256]{0:T(256)} %cdocs.1, s32[16]{0:T(128)} %ndocs.1, s32[32]{0:T(128)} %tiles.1, s32[1]{0:T(128)} %bitcast.place, bf16[8,64,2048]{2,1,0:T(8,128)(2,1)} %get-tuple-element.11.q_hbm, bf16[8704,128]{1,0:T(8,128)(2,1)} %bitcast.4), custom_call_target="tpu_custom_call" | custom-call | tf_op jit(solution)/shard_map/attention/pallas_call | solution.py:186
  57.0 1.3 collective-permute-done.whi
  58.3 0.0 copy-start
  58.3 1.1 copy-done
  59.4 69.9 %project.1 = bf16[512,512]{1,0:T(8,128)(2,1)} custom-call(bf16[2,4,64,2048]{3,2,1,0:T(8,128)(2,1)} %bitcast.5, f32[2,4,64,128]{3,2,1,0:T(8,128)} %bitcast.6, bf16[2048,512]{1,0:T(8,128)(2,1)} %w.3, bf16[768,512]{1,0:T(8,128)(2,1)} %get-tuple-element.15.wlo, bf16[1280,512]{1,0:T(8,128)(2,1)} %copy-done), custom_call_target="tpu_custom_call" | custom-call | tf_op jit(solution)/shard_map/project/pallas_call | solution.py:558
  129.3 1.9 %copy.11 = bf16[512,512]{1,0:T(8,128)(2,1)} copy(bf16[512,512]{1,0:T(8,128)(2,1)} %project.1) | data formatting | bytes 1048576
Async XLA Ops:
  29.3 29.0 %collective-permute-start = (bf16[1280,512]{1,0:T(8,128)(2,1)}, bf16[1280,512]{1,0:T(8,128)(2,1)S(1)}, u32[]{:S(2)}, u32[]{:S(2)}) collective-permute-start(bf16[1280,512]{1,0:T(8,128)(2,1)} %get-tuple-element.16), channel_id=1, source_target_pairs={{0,64},{4,68},{8,72},{12,76},{16,80},{20,84},{24,88},{28,92},{32,9... | collective-permute-start | bytes 3932168 | tf_op jit(solution)/shard_map/ppermute | solution.py:584
  58.3 1.1 copy-start

commit v3 on v2

--- a/solution.py
+++ b/solution.py
@@ -12,30 +12,53 @@
 SUB=1024
 
 def attn_kernel(cdocs, ndocs, tiles, place, q_hbm, kv_hbm, o_hbm, st_hbm, q_ref, kv_ref, o_ref, st_ref,
-                q_s, m_s, l_s, acc_s, lst, sems, *, nb):
+                q_s, m_s, l_s, acc_s, top_s, lst, cnt, sems, *, nb):
     q_in = lambda g: pltpu.make_async_copy(q_hbm.at[g], q_ref.at[g], sems.at[0, g])
     o_out = lambda g: pltpu.make_async_copy(o_ref.at[g], o_hbm.at[g], sems.at[1, g])
     kv_in = pltpu.make_async_copy(kv_hbm, kv_ref, sems.at[2, 0])
-    st_out = pltpu.make_async_copy(st_ref, st_hbm, sems.at[2, 1])
+    st_out = pltpu.make_async_copy(st_ref, st_hbm.at[pl.ds(0, 8)], sems.at[2, 1])
     kv_in.start()
     for g in range(8):
         q_in(g).start()
+    c = place[0]
+    y = c % 4
+    for d in range(4):
+        cnt[d] = 0
+
+    def add(i, _):
+        d = cdocs[(c - y) * 8 + i]
+        n = cnt[d]
+        lst[d * 32 + n] = (i // 8) * MEM + (i % 8) * BLK
+        cnt[d] = n + 1
+        return 0
+    lax.fori_loop(0, 32, add, 0)
+    top_s[...] = jnp.zeros_like(top_s)
     kv_in.wait()
 
-    def run(g, _):
+    def run(g, careful):
+        attend_run(g, c, careful, cnt, ndocs, tiles, q_ref, kv_ref, o_ref, st_ref, q_s, m_s, l_s, acc_s, top_s, lst, nb)
+        o_out(g).start()
+
+    def fast(g, _):
         q_in(g).wait()
-        attend_run(g, cdocs, ndocs, tiles, place, q_ref, kv_ref, o_ref, st_ref, q_s, m_s, l_s, acc_s, lst, nb)
-        o_out(g).start()
+        run(g, False)
         return 0
-    lax.fori_loop(0, 8, run, 0)
+    lax.fori_loop(0, 8, fast, 0)
+
+    @pl.when(jnp.logical_not(jnp.max(top_s[...]) < 1e30))
+    def _():
+        def again(g, _):
+            o_out(g).wait()
+            run(g, True)
+            return 0
+        lax.fori_loop(0, 8, again, 0)
     st_out.start()
     for g in range(8):
         o_out(g).wait()
     st_out.wait()
 
 
-def attend_run(g, cdocs, ndocs, tiles, place, q_ref, kv_ref, o_ref, st_ref, q_s, m_s, l_s, acc_s, lst, nb):
-    c = place[0]
+def attend_run(g, c, careful, cnt, ndocs, tiles, q_ref, kv_ref, o_ref, st_ref, q_s, m_s, l_s, acc_s, top_s, lst, nb):
     y = c % 4
     src = g * 4 + y
     members = [c - y + i for i in range(4)]
@@ -43,142 +66,118 @@
     qd = ndocs[tq // 2]
     nrow = ROWS*HEADS
     for h in range(HEADS):
-        q_s[h*ROWS:(h+1)*ROWS, :] = q_ref[g, :, h*HD:(h+1)*HD]
-    m_s[...] = jnp.full_like(m_s, NEG)
+        part = q_ref[g, :, h*HD:(h+1)*HD]
+        q_s[h*ROWS:(h+1)*ROWS, :HD] = part
+        q_s[h*ROWS:(h+1)*ROWS, HD:] = part
+    if careful:
+        m_s[...] = jnp.full_like(m_s, NEG)
     l_s[...] = jnp.zeros_like(l_s)
     acc_s[...] = jnp.zeros_like(acc_s)
-    n = jnp.int32(0)
-    for mi, c in enumerate(members):
-        def add(b, n):
-            ok = cdocs[c*8 + b] == qd
-            lst[n] = mi*MEM + b*BLK
-            return n + ok.astype(jnp.int32)
-        n = lax.fori_loop(0, 8, add, n)
-
-    def slow_step(kc, vc, mask_fn):
-        for t in range(nrow//SUB):
-            r = pl.ds(t*SUB, SUB)
-            s = lax.dot_general(q_s[r, :], kc, (((1,),(1,)),((),())), preferred_element_type=jnp.float32)
-            if mask_fn is not None:
-                s = mask_fn(s)
-            w = s.shape[1]//128
-            mx = s[:, :128]
-            for i in range(1, w):
-                mx = jnp.maximum(mx, s[:, i*128:(i+1)*128])
-            mx = jnp.max(mx, axis=1, keepdims=True)
-            m_old = m_s[r, :]
-            m_new = jnp.maximum(m_old, mx)
-            alpha = jnp.exp2((m_old - m_new)*(SCALE*L2E))
-            p = [jnp.exp2((s[:, i*128:(i+1)*128] - m_new)*(SCALE*L2E)) for i in range(w)]
-            ps = p[0]
-            for i in range(1, w):
-                ps = ps + p[i]
-            l_s[r, :] = l_s[r, :]*alpha + ps
-            m_s[r, :] = m_new
-            pb = jnp.concatenate([x.astype(jnp.bfloat16) for x in p], axis=1)
-            acc_s[r, :] = acc_s[r, :]*alpha + jnp.dot(pb, vc, preferred_element_type=jnp.float32)
-
-
-    def peak(kc, mask_fn):
-        for t in range(nrow//SUB):
-            r = pl.ds(t*SUB, SUB)
-            s = lax.dot_general(q_s[r, :], kc, (((1,),(1,)),((),())), preferred_element_type=jnp.float32)
-            if mask_fn is not None:
-                s = mask_fn(s)
-            w = s.shape[1]//128
-            mx = s[:, :128]
-            for i in range(1, w):
-                mx = jnp.maximum(mx, s[:, i*128:(i+1)*128])
-            m_s[r, :] = jnp.broadcast_to(jnp.max(mx, axis=1, keepdims=True), (SUB, 128))
-
-    def step(kc, vc, mask_fn):
-        for t in range(nrow//SUB):
-            r = pl.ds(t*SUB, SUB)
-            s = lax.dot_general(q_s[r, :], kc, (((1,),(1,)),((),())), preferred_element_type=jnp.float32)
-            if mask_fn is not None:
-                s = mask_fn(s)
-            w = s.shape[1]//128
-            m = m_s[r, :]
-            p = [jnp.exp2((s[:, i*128:(i+1)*128] - m)*(SCALE*L2E)) for i in range(w)]
-            ps = p[0]
-            for i in range(1, w):
-                ps = ps + p[i]
-            l_s[r, :] = l_s[r, :] + ps
-            pb = jnp.concatenate([x.astype(jnp.bfloat16) for x in p], axis=1)
-            acc_s[r, :] = acc_s[r, :] + jnp.dot(pb, vc, preferred_element_type=jnp.float32)
+    n = cnt[qd]
+    first = qd * 32
+
+    def scores(kc, masked):
+        k2 = jnp.concatenate([kc, jnp.broadcast_to(-base, kc.shape)], axis=1)
+        s = lax.dot_general(q_s[...], k2, (((1,),(1,)),((),())), preferred_element_type=jnp.float32)
+        tiles_of = [s[:, i*128:(i+1)*128] for i in range(s.shape[1]//128)]
+        return tiles_of[:-2] + mask(tiles_of[-2:]) if masked else tiles_of
+
+    def step(kc, vc, masked):
+        s = scores(kc, masked)
+        if careful:
+            m_old = m_s[...]
+            m = jnp.maximum(m_old, jnp.max(functools.reduce(jnp.maximum, s), axis=1, keepdims=True))
+            alpha = jnp.exp2((m_old - m)*(SCALE*L2E))
+            l_s[...] = l_s[...]*alpha
+            acc_s[...] = acc_s[...]*alpha
+            m_s[...] = m
+            s = [a - m for a in s]
+        p = [jnp.exp2(a*(SCALE*L2E)) for a in s]
+        l_s[...] = l_s[...] + functools.reduce(jnp.add, p)
+        pb = jnp.concatenate([a.astype(jnp.bfloat16) for a in p], axis=1)
+        acc_s[...] = acc_s[...] + jnp.dot(pb, vc, preferred_element_type=jnp.float32)
 
     def at(off, rows=BLK):
         return kv_ref[pl.ds(pl.multiple_of(off, 64), rows), :]
 
-    def chunks(step):
-        def chunk(base, size):
-            offs = [lst[base + j] for j in range(size)]
-            kc = jnp.concatenate([at(o) for o in offs], axis=0)
-            vc = jnp.concatenate([at(o + HALF) for o in offs], axis=0)
-            step(kc, vc, None)
-        def body(i, _):
-            chunk(i*nb, nb)
-            return 0
-        lax.fori_loop(0, n // nb, body, 0)
-        size = nb // 2
-        while size >= 1:
-            @pl.when((n // size) % 2 == 1)
-            def _(size=size):
-                chunk((n // (2*size))*(2*size), size)
-            size //= 2
-    kcs = []; vcs = []
     newlims = []
-    for mi, c in enumerate(members):
-        tk = tiles[c]
-        same_doc = ndocs[tk // 2] == qd
-        full_ok = same_doc & (tk < tq)
+    new_k, new_v = [], []
+    for mi, cm in enumerate(members):
+        tk = tiles[cm]
+        full_ok = (ndocs[tk // 2] == qd) & (tk < tq)
         diag = tk == tq
         newlims.append((jnp.where(full_ok, 1 << 20, jnp.where(diag, 0, -1)), jnp.where(diag, 1, 0)))
-        kcs.append(kv_ref[mi*MEM + CR: mi*MEM + HALF, :])
-        vcs.append(kv_ref[mi*MEM + HALF + CR: (mi+1)*MEM, :])
-    kc = jnp.concatenate(kcs, axis=0); vc = jnp.concatenate(vcs, axis=0)
+        new_k.append(kv_ref[mi*MEM + CR: mi*MEM + HALF, :])
+        new_v.append(kv_ref[mi*MEM + HALF + CR: (mi+1)*MEM, :])
     any_new = functools.reduce(jnp.logical_or, [lim >= 0 for lim, _ in newlims])
-    def mask(s):
-        row = lax.broadcasted_iota(jnp.int32, (SUB, 128), 0) % ROWS
-        lane = lax.broadcasted_iota(jnp.int32, (SUB, 128), 1)
+    where = jnp.int32(0)
+    for mi in range(4):
+        where = jnp.where(newlims[mi][0] >= 0, mi*MEM + CR, where)
+    where = jnp.where(n > 0, lst[first], where)
+    base = at(where, 16)[0:1, :]
+
+    def mask(pair):
+        row = lax.broadcasted_iota(jnp.int32, (nrow, 128), 0) % ROWS
+        lane = lax.broadcasted_iota(jnp.int32, (nrow, 128), 1)
         out = []
         for a in range(2):
             (b0, d0), (b1, d1) = newlims[2*a], newlims[2*a+1]
-            lo = row*d0 + b0
-            hi = row*d1 + b1
-            ok = lane <= jnp.where(lane < ROWS, lo, hi + ROWS)
-            k0 = a*128
-            out.append(jnp.where(ok, s[:, k0:k0+128], NEG))
-        return jnp.concatenate(out, axis=1)
-    @pl.when(n > 0)
-    def _():
-        peak(at(lst[0]), None)
-    @pl.when((n == 0) & any_new)
-    def _():
-        peak(kc, mask)
-    chunks(step)
-    @pl.when(any_new)
-    def _():
-        step(kc, vc, mask)
-    @pl.when(jnp.logical_not(jnp.max(l_s[...]) < 1e30))
-    def _():
-        m_s[...] = jnp.full_like(m_s, NEG)
-        l_s[...] = jnp.zeros_like(l_s)
-        acc_s[...] = jnp.zeros_like(acc_s)
-        chunks(slow_step)
+            ok = lane <= jnp.where(lane < ROWS, row*d0 + b0, row*d1 + b1 + ROWS)
+            out.append(jnp.where(ok, pair[a], NEG))
+        return out
+
+    def chunk(base, size, with_new=False):
+        offs = [lst[first + base + j] for j in range(size)]
+        kc = jnp.concatenate([at(o) for o in offs] + (new_k if with_new else []), axis=0)
+        vc = jnp.concatenate([at(o + HALF) for o in offs] + (new_v if with_new else []), axis=0)
+        step(kc, vc, with_new)
+
+    if careful:
+        def body(i, _):
+            chunk(i, 1)
+            return 0
+        lax.fori_loop(0, n, body, 0)
+
         @pl.when(any_new)
         def _():
-            slow_step(kc, vc, mask)
+            chunk(0, 0, True)
+    else:
+        def body(i, _):
+            chunk(i*2*nb, 2*nb)
+            return 0
+        lax.fori_loop(0, n // (2*nb), body, 0)
+
+        @pl.when((n // nb) % 2 == 1)
+        def _():
+            chunk(n // (2*nb) * (2*nb), nb)
+        for left in range(nb):
+            @pl.when(any_new & (n % nb == left))
+            def _(left=left):
+                chunk(n - left, left, True)
+
+            if left:
+                @pl.when(jnp.logical_not(any_new) & (n % nb == left))
+                def _(left=left):
+                    chunk(n - left, left)
     lane = lax.broadcasted_iota(jnp.int32, (ROWS, 128), 1)
     st = jnp.full((ROWS, 128), NEG, jnp.float32)
+    top = top_s[...]
+    peaks = lax.dot_general(q_s[:, :HD], jnp.broadcast_to(base, (128, HD)), (((1,),(1,)),((),())),
+                            preferred_element_type=jnp.float32)
     for h in range(HEADS):
         r = pl.ds(h*ROWS, ROWS)
         l = jnp.sum(l_s[r, :], axis=1, keepdims=True)
-        l = jnp.maximum(l, 1e-30)
-        o_ref[g, :, h*HD:(h+1)*HD] = (acc_s[r, :] / l).astype(jnp.bfloat16)
-        lse = m_s[r, :]*SCALE + jnp.log(l)
-        st = jnp.where(lane == h, lse, st)
+        top = jnp.maximum(top, l)
+        some = l > 0.0
+        l = jnp.where(some, l, 1.0)
+        o_ref[g, :, h*HD:(h+1)*HD] = (acc_s[r, :] * (1.0 / l)).astype(jnp.bfloat16)
+        peak = peaks[h*ROWS:(h+1)*ROWS]
+        if careful:
+            peak = peak + m_s[r, :]
+        st = jnp.where(lane == h, jnp.where(some, peak*SCALE + jnp.log(l), NEG), st)
     st_ref[g] = st
+    top_s[...] = top
+
 
 def attention(qg, kvg, cdocs, ndocs, tiles, place, nb=4):
     nrow = ROWS*HEADS
@@ -189,18 +188,20 @@
         out_specs=[anywhere] * 2,
         scratch_shapes=[pltpu.VMEM((8, ROWS, HEADS*HD), jnp.bfloat16), pltpu.VMEM((4*MEM, HD), jnp.bfloat16),
                         pltpu.VMEM((8, ROWS, HEADS*HD), jnp.bfloat16), pltpu.VMEM((8, ROWS, 128), jnp.float32),
-                        pltpu.VMEM((nrow, HD), jnp.bfloat16), pltpu.VMEM((nrow, 128), jnp.float32),
+                        pltpu.VMEM((nrow, 2*HD), jnp.bfloat16), pltpu.VMEM((nrow, 128), jnp.float32),
                         pltpu.VMEM((nrow, 128), jnp.float32), pltpu.VMEM((nrow, HD), jnp.float32),
-                        pltpu.SMEM((40,), jnp.int32), pltpu.SemaphoreType.DMA((3, 8))],
+                        pltpu.VMEM((ROWS, 128), jnp.float32),
+                        pltpu.SMEM((128,), jnp.int32), pltpu.SMEM((4,), jnp.int32), pltpu.SemaphoreType.DMA((3, 8))],
         out_shape=[jax.ShapeDtypeStruct((8, ROWS, HEADS*HD), jnp.bfloat16),
-                   jax.ShapeDtypeStruct((8, ROWS, 128), jnp.float32)],
-        compiler_params=pltpu.CompilerParams(vmem_limit_bytes=56 << 20),
+                   jax.ShapeDtypeStruct((24, ROWS, 128), jnp.float32)],
+        compiler_params=pltpu.CompilerParams(vmem_limit_bytes=(64 << 20) - (512 << 10)),
         name="attention",
     )(cdocs, ndocs, tiles, place, qg, kvg)
 
 
 MESH = pl.DeviceIdType.MESH
 WROWS = 768
+WMID = 1664
 
 
 def coords():
@@ -249,7 +250,7 @@
     for i, (src, off, n) in enumerate(pieces):
         locs.append(pltpu.make_async_copy(src, kvg.at[y, pl.ds(off, n)], lsem.at[1 + i]))
     locs.append(pltpu.make_async_copy(w.at[pl.ds(0, WROWS)], ws, lsem.at[5]))
-    locs.append(pltpu.make_async_copy(w.at[pl.ds(WROWS, 2048 - WROWS)], wr, lsem.at[6]))
+    locs.append(pltpu.make_async_copy(w.at[pl.ds(WROWS, WMID - WROWS)], wr, lsem.at[6]))
     for cp in locs:
         cp.start()
     greet([to_yr, to_yl, to_xr, to_xl, to_z])
@@ -328,9 +329,9 @@
         out_shape=[jax.ShapeDtypeStruct((8, ROWS, HEADS * HD), jnp.bfloat16),
                    jax.ShapeDtypeStruct((4, MEM, HD), jnp.bfloat16),
                    jax.ShapeDtypeStruct((WROWS, 512), jnp.bfloat16),
-                   jax.ShapeDtypeStruct((2048 - WROWS, 512), jnp.bfloat16)],
+                   jax.ShapeDtypeStruct((WMID - WROWS, 512), jnp.bfloat16)],
         scratch_shapes=[pltpu.VMEM((8, ROWS, HEADS * HD), bf), pltpu.VMEM((4, MEM, HD), bf), pltpu.VMEM((WROWS, 512), bf),
-                        pltpu.VMEM((2048 - WROWS, 512), bf), pltpu.VMEM((WROWS, 512), bf), pltpu.SemaphoreType.DMA((20,)),
+                        pltpu.VMEM((WMID - WROWS, 512), bf), pltpu.VMEM((WROWS, 512), bf), pltpu.SemaphoreType.DMA((20,)),
                         pltpu.SemaphoreType.DMA((20,)), pltpu.SemaphoreType.DMA((7,)), pltpu.SemaphoreType.DMA((14,))],
         compiler_params=pltpu.CompilerParams(collective_id=0, has_side_effects=True, vmem_limit_bytes=56 << 20),
         name="gather",
@@ -371,7 +372,7 @@
     to_yr, to_yl, to_xr, to_xl = dev(z, x, yr), dev(z, x, yl), dev(z, xr, y), dev(z, xl, y)
     to_z = dev(zp, x, y)
     to_x = lambda d: dev(z, (x + d) % 4, y)
-    ready = [pltpu.make_async_copy(o_hbm, o, lsem.at[3]), pltpu.make_async_copy(st_hbm, st, lsem.at[4])]
+    ready = [pltpu.make_async_copy(o_hbm, o, lsem.at[3]), pltpu.make_async_copy(st_hbm.at[pl.ds(0, 2)], st, lsem.at[4])]
     for cp in ready:
         cp.start()
     greet([to_xr, to_xl, to_x(2), to_z, to_yr, to_yl, core, zdev(0, 1 - h), zdev(1, 1 - h)])
@@ -390,7 +391,7 @@
         outs.append(send(o.at[:, xx, lo], px.at[x], (a_s.at[0], a_r.at[0]), d, to_x(d)))
     weights = [pltpu.make_async_copy(w, w_s.at[z], lsem.at[0]),
                pltpu.make_async_copy(wlo, w_s.at[zp, pl.ds(0, WROWS)], lsem.at[1]),
-               pltpu.make_async_copy(whi, w_s.at[zp, pl.ds(WROWS, 2048 - WROWS)], lsem.at[2])]
+               pltpu.make_async_copy(whi, w_s.at[zp, pl.ds(WROWS, WMID - WROWS)], lsem.at[2])]
     for cp in weights:
         cp.start()
     for d in (2, 1, 3, 0):
@@ -417,6 +418,9 @@
     nz[...] = lse
     outs.append(send(nz, tz, (c_s, c_r), 1, to_z))
     outs.append(send(mz, rz, (c_s, c_r), 0, to_z))
+    weights[0].wait()
+    far = pl.ds(WMID, 2048 - WMID)
+    outs.append(send(w_s.at[z, far], w_s.at[z, far], (c_s, c_r), 2, to_z))
     own_cols, own_lse = merge([o[z, x, 0:32, :]] + [px[xx, z] for xx in others],
                               [st[z, x, 0:32, :]] + [sx[xx, z] for xx in others])
     mine = x * 4 + y
@@ -475,77 +479,110 @@
     for hf in (0, 1):
         last(hf, 0, 0, 0)
         both(hf, 1, 2, 16)
-    for a, i in ((0, 4), (3, 8), (1, 12), (2, 16)):
-        for hf in (0, 1):
-            relay(hf, 1, a, i)
-    for cp in weights:
-        cp.wait()
-
-    def places(p):
-        hf, late = p % 2, p // 2
+
+    near, sides, beyond = (0,), (1, 3), (2,)
+    pieces = [(0, near), (0, sides), (1, 1), (1, 0), (0, beyond)]
+    counts = [64, 128, 128, 128, 64]
+
+    def places(p, kk):
+        hf, what = pieces[p]
         if hf == 0:
-            first = [(2 * (1 - k) + i, (y + n) % 4) for i in (0, 1) for n in ((1, 3), (0, 2))[late]]
-            then = [(2 * k + i, (y + n) % 4) for i in (0, 1) for n in ((1, 3), (0, 2))[late]]
-        else:
-            parity = (x + 1 - late) % 2
-            first = [(2 * (1 - k) + parity, n) for n in range(4)]
-            then = [(2 * k + parity, n) for n in range(4)]
-        return hf, first, then
+            return [(2 * kk + i, (y + n) % 4) for i in (0, 1) for n in what]
+        return [(2 * kk + (x + what) % 2, n) for n in range(4)]
+
+    def rows_of(hf, blocks):
+        return [attg[slot(*s), 32 * hf:32 * hf + 32, :] for s in blocks]
+
+    def product(lhs, b):
+        return jnp.dot(jnp.concatenate(lhs, axis=0), w_s[b], preferred_element_type=jnp.float32)
 
     mine_at = lambda b: (h == z) & (b == z)
+    part_of = lambda p: pl.ds(0, counts[p])
+
+    def to_core(p):
+        outs.append(send(ct.at[p, :, part_of(p)], cr.at[p, :, part_of(p)], (cs, crs), p, core))
 
     def multiply(p):
-        hf, first, then = places(p)
-        lhs = jnp.concatenate([attg[slot(*s), 32 * hf:32 * hf + 32, :] for s in first + then], axis=0)
+        n = counts[p]
+        lhs = rows_of(pieces[p][0], places(p, 1 - k) + places(p, k))
         for b in (0, 1):
-            r = jnp.dot(lhs, w_s[b], preferred_element_type=jnp.float32)
-            ct[p, b] = r[:128].astype(jnp.bfloat16)
-            acc[p, b] = r[128:]
-        outs.append(send(ct.at[p], cr.at[p], (cs, crs), p, core))
+            r = product(lhs, b)
+            ct[p, b, :n] = r[:n].astype(jnp.bfloat16)
+            acc[p, b, :n] = r[n:]
+        to_core(p)
 
     def exchange(p):
-        arrive(cr.at[p], (cs, crs), p, core)
+        n = counts[p]
+        arrive(cr.at[p, :, part_of(p)], (cs, crs), p, core)
         for b in (0, 1):
-            zt[p, b] = (acc[p, b] + cr[p, b].astype(jnp.float32)).astype(jnp.bfloat16)
+            zt[p, b, :n] = (acc[p, b, :n] + cr[p, b, :n].astype(jnp.float32)).astype(jnp.bfloat16)
 
             @pl.when(jnp.logical_not(mine_at(b)))
             def _():
-                send(zt.at[p, b], zr.at[h, p], (zs, zrs.at[h]), p * 2 + b, zdev(b, z))
+                send(zt.at[p, b, part_of(p)], zr.at[h, p, part_of(p)], (zs, zrs.at[h]), p * 2 + b, zdev(b, z))
 
             @pl.when(mine_at(b))
             def _():
-                zr[h, p] = zt[p, b]
-
-    multiply(0)
+                zr[h, p, :n] = zt[p, b, :n]
+
+    for hf in (0, 1):
+        relay(hf, 1, 0, 4)
+    for cp in weights[1:]:
+        cp.wait()
+    arrive(w_s.at[zp, far], (c_s, c_r), 2, to_z)
+    lhs = rows_of(0, places(0, 1 - k) + places(0, k)) + rows_of(1, [(x, n) for n in range(4)])
+    for b in (0, 1):
+        r = product(lhs, b)
+        ct[0, b, :64] = r[:64].astype(jnp.bfloat16)
+        acc[0, b, :64] = r[64:128]
+        acc[3, b] = r[128:]
+    to_core(0)
+    for hf in (0, 1):
+        relay(hf, 1, 3, 8)
+    for hf in (0, 1):
+        relay(hf, 1, 1, 12)
+    exchange(0)
+    for hf in (0, 1):
+        relay(hf, 1, 2, 16)
     multiply(1)
-    exchange(0)
+    multiply(2)
     exchange(1)
-    for a, i in ((0, 4), (3, 8), (1, 12), (2, 16)):
-        for hf in (0, 1):
+    exchange(2)
+    for hf in (0, 1):
+        for a, i in ((0, 4), (3, 8), (1, 12), (2, 16)):
             last(hf, 1, a, i)
-    multiply(2)
-    multiply(3)
-    exchange(2)
+    here = (x // 2) == k
+    lhs = rows_of(0, places(4, 1 - k) + places(4, k)) + rows_of(1, [((x + 2) % 4, n) for n in range(4)])
+    for b in (0, 1):
+        r = product(lhs, b)
+        ct[4, b, :64] = r[:64].astype(jnp.bfloat16)
+        acc[4, b, :64] = r[64:128]
+        early, late = acc[3, b], r[128:]
+        ct[3, b] = jnp.where(here, late, early).astype(jnp.bfloat16)
+        acc[3, b] = jnp.where(here, early, late)
+    to_core(3)
+    to_core(4)
     exchange(3)
-    for p in range(4):
+    exchange(4)
+    for p in range(5):
+        n = counts[p]
         for s in (0, 1):
             @pl.when(jnp.logical_not((s == h) & (z == h)))
             def _():
                 pltpu.make_async_remote_copy(
-                    src_ref=zr.at[s, p], dst_ref=zr.at[s, p], send_sem=zs.at[0], recv_sem=zrs.at[s, p * 2 + z],
-                    device_id=zdev(h, s), device_id_type=MESH).wait_recv()
-        total = (zr[0, p].astype(jnp.float32) + zr[1, p].astype(jnp.float32)).astype(jnp.bfloat16)
-        hf, _, then = places(p)
-        for i, (xx, yy) in enumerate(then):
-            off = (slot(xx, yy) - 8 * k) * 64 + 32 * hf
+                    src_ref=zr.at[s, p, part_of(p)], dst_ref=zr.at[s, p, part_of(p)], send_sem=zs.at[0],
+                    recv_sem=zrs.at[s, p * 2 + z], device_id=zdev(h, s), device_id_type=MESH).wait_recv()
+        total = (zr[0, p, :n].astype(jnp.float32) + zr[1, p, :n].astype(jnp.float32)).astype(jnp.bfloat16)
+        for i, (xx, yy) in enumerate(places(p, k)):
+            off = (slot(xx, yy) - 8 * k) * 64 + 32 * pieces[p][0]
             out[pl.ds(pl.multiple_of(off, 32), 32), :] = total[32 * i:32 * i + 32]
-    for p in range(4):
+    for p in range(5):
         for b in (0, 1):
             @pl.when(jnp.logical_not(mine_at(b)))
             def _():
                 pltpu.make_async_remote_copy(
-                    src_ref=zt.at[p, b], dst_ref=zt.at[p, b], send_sem=zs.at[p * 2 + b], recv_sem=zrs.at[0, 0],
-                    device_id=zdev(b, z), device_id_type=MESH).wait_send()
+                    src_ref=zt.at[p, b, part_of(p)], dst_ref=zt.at[p, b, part_of(p)], send_sem=zs.at[p * 2 + b],
+                    recv_sem=zrs.at[0, 0], device_id=zdev(b, z), device_id_type=MESH).wait_send()
     for cp in outs:
         cp.wait_send()
 
@@ -569,12 +606,12 @@
             pltpu.VMEM((3, 32, wide), bf), pltpu.VMEM((3, 32, 128), f32),
             pltpu.VMEM((4, 32, wide), bf), pltpu.VMEM((4, 32, 128), f32),
             pltpu.VMEM((16, ROWS, wide), bf), pltpu.VMEM((2, 2048, 512), bf),
-            pltpu.VMEM((4, 2, 128, 512), bf), pltpu.VMEM((4, 2, 128, 512), bf), pltpu.VMEM((4, 2, 128, 512), f32),
-            pltpu.VMEM((4, 2, 128, 512), bf), pltpu.VMEM((2, 4, 128, 512), bf),
-            dma((2, 4)), dma((2, 4)), dma((2, 4)), dma((2, 4)), dma((2,)), dma((2,)), dma((2, 4)), dma((2, 4)),
-            dma((2, 20)), dma((2, 20)), dma((4,)), dma((4,)), dma((8,)), dma((2, 8)), dma((5,)),
+            pltpu.VMEM((5, 2, 128, 512), bf), pltpu.VMEM((5, 2, 128, 512), bf), pltpu.VMEM((5, 2, 128, 512), f32),
+            pltpu.VMEM((5, 2, 128, 512), bf), pltpu.VMEM((2, 5, 128, 512), bf),
+            dma((2, 4)), dma((2, 4)), dma((2, 4)), dma((2, 4)), dma((3,)), dma((3,)), dma((2, 4)), dma((2, 4)),
+            dma((2, 20)), dma((2, 20)), dma((5,)), dma((5,)), dma((10,)), dma((2, 10)), dma((5,)),
         ],
-        compiler_params=pltpu.CompilerParams(collective_id=1, has_side_effects=True, vmem_limit_bytes=56 << 20),
+        compiler_params=pltpu.CompilerParams(collective_id=1, has_side_effects=True, vmem_limit_bytes=53 << 20),
         name="project",
     )(o, st, w, wlo, whi)
 
@@ -584,7 +621,7 @@
     whi = lax.ppermute(rest, "ctx", [(i, i ^ 16) for i in range(32)])
     place = jnp.reshape(lax.axis_index("ctx"), (1,)).astype(jnp.int32)
     o, st = attention(qg, kvg.reshape(4 * MEM, HD), cache_docs, new_docs, slot_tile, place)
-    return project(o.reshape(2, 4, ROWS, HEADS * HD), st.reshape(2, 4, ROWS, 128), out_weight, wlo, whi)
+    return project(o.reshape(2, 4, ROWS, HEADS * HD), st.reshape(6, 4, ROWS, 128), out_weight, wlo, whi)
 
 
 def solution(mesh):

time: 131 us -> 177 us (1.35)
  Pallas kernels: 127 us -> 176 us
  local copies, waits for them, and re-layouts: 2.93 us -> 0.8 us
    pallas_call x1, Pallas kernels: 27.6 us -> 56.9 us  [attention(): pl.pallas_call(functools.partial(attn_kernel, nb=nb), in_specs=[smem] * 4...]
    pallas_call x1, Pallas kernels: 69.9 us -> 89.7 us  [project(): pl.pallas_call(project_kernel, in_specs=[hbm] * 5, out_specs=vmem, out_sh...]
    unnamed x3 -> x1, local copies, waits for them, and re-layouts: 2.93 us -> 0.8 us
  transfers between devices with their start and end apart: 1 -> 1, of which waited for: 1 -> 0; matrix products, arithmetic and copies ran while one was open for 0% -> 0% of each run, Pallas kernels for 21% -> 32%
where the time goes in v3:
time: 177 us
  Pallas kernels  176 us (99%)
    pallas_call x1, Pallas kernels, project(): pl.pallas_call(project_kernel, in_specs=[hbm] * 5, out_specs=vmem, out_sh...  89.7 us
    pallas_call x1, Pallas kernels, attention(): pl.pallas_call(functools.partial(attn_kernel, nb=nb), in_specs=[smem] * 4...  56.9 us
    pallas_call x1, Pallas kernels, gather(): pl.pallas_call(gather_kernel, in_specs=[hbm] * 6, out_specs=[hbm] * 4, ou...  29.3 us
  transfers between devices with their start and end apart: 1, of which 0 were waited for; matrix products, arithmetic and copies ran while one was open for 0% of the time, Pallas kernels for 32%

profile of v3, /device:TPU:1, one launch (start us, length us, event | category | flops | bytes accessed | tf_op | source)
XLA Modules:
  0.0 176.8 jit_solution(7881870111563525046)
XLA Ops:
  0.0 29.3 %gather.1 = (bf16[8,64,2048]{2,1,0:T(8,128)(2,1)}, bf16[4,2176,128]{2,1,0:T(8,128)(2,1)}, bf16[768,512]{1,0:T(8,128)(2,1)}, bf16[896,512]{1,0:T(8,128)(2,1)}) custom-call(bf16[64,2048]{1,0:T(8,128)(2,1)} %q.1, bf16[1024,128]{1,0:T(8,128)(2,1)} %ck.1, bf16[1024,128]{1,0:T(8,128)(2,1)} %cv.1, bf16[64,128]{1,0:T(8,128)(2,1)} %nk.1, bf16[64,128]{1,0:T(8,128)(2,1)} %nv.1, ...), custom_call_target="tpu_custom_call" | custom-call | tf_op jit(solution)/shard_map/gather/pallas_call | solution.py:325
  29.3 0.1 collective-permute-start
  29.4 56.9 %attention.1 = (bf16[8,64,2048]{2,1,0:T(8,128)(2,1)}, f32[24,64,128]{2,1,0:T(8,128)}) custom-call(s32[256]{0:T(256)} %cdocs.1, s32[16]{0:T(128)} %ndocs.1, s32[32]{0:T(128)} %tiles.1, s32[1]{0:T(128)} %bitcast.place, bf16[8,64,2048]{2,1,0:T(8,128)(2,1)} %get-tuple-element.11.q_hbm, bf16[8704,128]{1,0:T(8,128)(2,1)} %bitcast.4), custom_call_target="tpu_custom_call" | custom-call | tf_op jit(solution)/shard_map/attention/pallas_call | solution.py:185
  86.3 0.0 collective-permute-done.whi
  86.3 89.7 %project.1 = bf16[512,512]{1,0:T(8,128)(2,1)S(1)} custom-call(bf16[2,4,64,2048]{3,2,1,0:T(8,128)(2,1)} %bitcast.5, f32[6,4,64,128]{3,2,1,0:T(8,128)} %bitcast.6, bf16[2048,512]{1,0:T(8,128)(2,1)} %w.3, bf16[768,512]{1,0:T(8,128)(2,1)} %get-tuple-element.15.wlo, bf16[896,512]{1,0:T(8,128)(2,1)} %collective-permute-done.whi), custom_call_target="tpu_custom_call" | custom-call | tf_op jit(solution)/shard_map/project/pallas_call | solution.py:595
  176.0 0.8 copy.11
Async XLA Ops:
  29.3 57.0 %collective-permute-start = (bf16[896,512]{1,0:T(8,128)(2,1)}, bf16[896,512]{1,0:T(8,128)(2,1)}, u32[]{:S(2)}, u32[]{:S(2)}) collective-permute-start(bf16[896,512]{1,0:T(8,128)(2,1)} %get-tuple-element.16), channel_id=1, source_target_pairs={{0,64},{4,68},{8,72},{12,76},{16,80},{20,84},{24,88},{28,92},{32,9... | collective-permute-start | bytes 2752520 | tf_op jit(solution)/shard_map/ppermute | solution.py:621

commit v4 on v3

--- a/solution.py
+++ b/solution.py
@@ -117,13 +117,14 @@
     base = at(where, 16)[0:1, :]
 
     def mask(pair):
-        row = lax.broadcasted_iota(jnp.int32, (nrow, 128), 0) % ROWS
-        lane = lax.broadcasted_iota(jnp.int32, (nrow, 128), 1)
+        row = lax.broadcasted_iota(jnp.int32, (ROWS, 128), 0)
+        lane = lax.broadcasted_iota(jnp.int32, (ROWS, 128), 1)
         out = []
         for a in range(2):
             (b0, d0), (b1, d1) = newlims[2*a], newlims[2*a+1]
             ok = lane <= jnp.where(lane < ROWS, row*d0 + b0, row*d1 + b1 + ROWS)
-            out.append(jnp.where(ok, pair[a], NEG))
+            bias = jnp.where(ok, 0.0, NEG)
+            out.append((pair[a].reshape(HEADS, ROWS, 128) + bias[None]).reshape(nrow, 128))
         return out
 
     def chunk(base, size, with_new=False):
@@ -200,8 +201,8 @@
 
 
 MESH = pl.DeviceIdType.MESH
-WROWS = 768
-WMID = 1664
+WROWS = 512
+WMID = 1600
 
 
 def coords():

time: 177 us -> 173 us (0.977)
  Pallas kernels: 176 us -> 170 us
    pallas_call x1, Pallas kernels: 89.7 us -> 77.3 us  [project(): pl.pallas_call(project_kernel, in_specs=[hbm] * 5, out_specs=vmem, out_sh...]
    pallas_call x1, Pallas kernels: 56.9 us -> 67.2 us  [attention(): pl.pallas_call(functools.partial(attn_kernel, nb=nb), in_specs=[smem] * 4...]
    pallas_call x1, Pallas kernels: 29.3 us -> 25.6 us  [gather(): pl.pallas_call(gather_kernel, in_specs=[hbm] * 6, out_specs=[hbm] * 4, ou...]
  transfers between devices with their start and end apart: 1 -> 1, of which waited for: 0 -> 0; matrix products, arithmetic and copies ran while one was open for 0% -> 0% of each run, Pallas kernels for 32% -> 39%
where the time goes in v4:
time: 173 us
  Pallas kernels  170 us (98%)
    pallas_call x1, Pallas kernels, project(): pl.pallas_call(project_kernel, in_specs=[hbm] * 5, out_specs=vmem, out_sh...  77.3 us
    pallas_call x1, Pallas kernels, attention(): pl.pallas_call(functools.partial(attn_kernel, nb=nb), in_specs=[smem] * 4...  67.2 us
    pallas_call x1, Pallas kernels, gather(): pl.pallas_call(gather_kernel, in_specs=[hbm] * 6, out_specs=[hbm] * 4, ou...  25.6 us
  transfers between devices with their start and end apart: 1, of which 0 were waited for; matrix products, arithmetic and copies ran while one was open for 0% of the time, Pallas kernels for 39%

profile of v4, /device:TPU:1, one launch (start us, length us, event | category | flops | bytes accessed | tf_op | source)
XLA Modules:
  0.0 172.6 jit_solution(7831024547436264776)
XLA Ops:
  0.0 25.6 %gather.1 = (bf16[8,64,2048]{2,1,0:T(8,128)(2,1)}, bf16[4,2176,128]{2,1,0:T(8,128)(2,1)}, bf16[512,512]{1,0:T(8,128)(2,1)}, bf16[1088,512]{1,0:T(8,128)(2,1)}) custom-call(bf16[64,2048]{1,0:T(8,128)(2,1)} %q.1, bf16[1024,128]{1,0:T(8,128)(2,1)} %ck.1, bf16[1024,128]{1,0:T(8,128)(2,1)} %cv.1, bf16[64,128]{1,0:T(8,128)(2,1)} %nk.1, bf16[64,128]{1,0:T(8,128)(2,1)} %nv.1, ...), custom_call_target="tpu_custom_call" | custom-call | tf_op jit(solution)/shard_map/gather/pallas_call | solution.py:326
  25.6 1.7 collective-permute-start
  27.3 67.2 %attention.1 = (bf16[8,64,2048]{2,1,0:T(8,128)(2,1)}, f32[24,64,128]{2,1,0:T(8,128)}) custom-call(s32[256]{0:T(256)} %cdocs.1, s32[16]{0:T(128)} %ndocs.1, s32[32]{0:T(128)} %tiles.1, s32[1]{0:T(128)} %bitcast.place, bf16[8,64,2048]{2,1,0:T(8,128)(2,1)} %get-tuple-element.11.q_hbm, bf16[8704,128]{1,0:T(8,128)(2,1)} %bitcast.4), custom_call_target="tpu_custom_call" | custom-call | tf_op jit(solution)/shard_map/attention/pallas_call | solution.py:186
  94.6 0.0 collective-permute-done.whi
  94.6 77.3 %project.1 = bf16[512,512]{1,0:T(8,128)(2,1)S(1)} custom-call(bf16[2,4,64,2048]{3,2,1,0:T(8,128)(2,1)} %bitcast.5, f32[6,4,64,128]{3,2,1,0:T(8,128)} %bitcast.6, bf16[2048,512]{1,0:T(8,128)(2,1)} %w.3, bf16[512,512]{1,0:T(8,128)(2,1)} %get-tuple-element.15.wlo, bf16[1088,512]{1,0:T(8,128)(2,1)} %collective-permute-done.whi), custom_call_target="tpu_custom_call" | custom-call | tf_op jit(solution)/shard_map/project/pallas_call | solution.py:596
  171.8 0.8 copy.11
Async XLA Ops:
  25.6 69.0 %collective-permute-start = (bf16[1088,512]{1,0:T(8,128)(2,1)}, bf16[1088,512]{1,0:T(8,128)(2,1)}, u32[]{:S(2)}, u32[]{:S(2)}) collective-permute-start(bf16[1088,512]{1,0:T(8,128)(2,1)} %get-tuple-element.16), channel_id=1, source_target_pairs={{0,64},{4,68},{8,72},{12,76},{16,80},{20,84},{24,88},{28,92},{32,9... | collective-permute-start | bytes 3342344 | tf_op jit(solution)/shard_map/ppermute | solution.py:622

commit v5 on v4

--- a/solution.py
+++ b/solution.py
@@ -355,13 +355,26 @@
     return cols, largest + jnp.log(total)
 
 
+def pack(stats):
+    lane = lax.broadcasted_iota(jnp.int32, (8, 128), 1)
+    out = None
+    for i in range(4 * len(stats)):
+        a = stats[i // 4][8 * (i % 4):8 * (i % 4) + 8]
+        out = a if i == 0 else jnp.where(lane >= 16 * i, pltpu.roll(a, 16 * i, 1), out)
+    return out
+
+
+def unpack(packed, i=0):
+    return jnp.concatenate([packed if i + g == 0 else pltpu.roll(packed, 128 - 64 * i - 16 * g, 1) for g in range(4)], axis=0)
+
+
 def put(ref, cols):
     for head, a in enumerate(cols):
         ref[:, head * HD:(head + 1) * HD] = a
 
 
 def project_kernel(o_hbm, st_hbm, w, wlo, whi, out, o, st, px, sx, pz, sz, mz, nz, rz, tz, mx, nx, rx, tx_s, attg, w_s, ct, cr, acc, zt, zr,
-                   a_s, a_r, b_s, b_r, c_s, c_r, d_s, d_r, gs, gr, cs, crs, zs, zrs, lsem):
+                   a_s, a_r, b_s, b_r, c_s, c_r, d_s, d_r, gs, gr, cs, crs, zs, zrs, lsem, sp):
     z, x, y = coords()
     t = lax.axis_index("tp")
     h, k = t // 2, t % 2
@@ -384,12 +397,18 @@
         cp.wait()
     for d in (2, 1, 3, 0):
         xx = (x + d) % 4
-        outs.append(send(st.at[zp, xx, hi], sz.at[xx], (b_s.at[1], b_r.at[1]), d, to_z))
         outs.append(send(o.at[zp, xx, hi], pz.at[xx], (b_s.at[0], b_r.at[0]), d, to_z))
     for d in (2, 1, 3):
         xx = (x + d) % 4
-        outs.append(send(st.at[:, xx, lo], sx.at[x], (a_s.at[1], a_r.at[1]), d, to_x(d)))
         outs.append(send(o.at[:, xx, lo], px.at[x], (a_s.at[0], a_r.at[0]), d, to_x(d)))
+    for d in (2, 1, 3, 0):
+        xx = (x + d) % 4
+        sp[0, d] = pack([st[zp, xx, 32:64, :]])
+        outs.append(send(sp.at[0, d], sz.at[xx], (b_s.at[1], b_r.at[1]), d, to_z))
+    for d in (2, 1, 3):
+        xx = (x + d) % 4
+        sp[1, d] = pack([st[0, xx, 0:32, :], st[1, xx, 0:32, :]])
+        outs.append(send(sp.at[1, d], sx.at[x], (a_s.at[1], a_r.at[1]), d, to_x(d)))
     weights = [pltpu.make_async_copy(w, w_s.at[z], lsem.at[0]),
                pltpu.make_async_copy(wlo, w_s.at[zp, pl.ds(0, WROWS)], lsem.at[1]),
                pltpu.make_async_copy(whi, w_s.at[zp, pl.ds(WROWS, WMID - WROWS)], lsem.at[2])]
@@ -399,13 +418,13 @@
         xx = (x + d) % 4
         arrive(sz.at[xx], (b_s.at[1], b_r.at[1]), d, to_z)
         arrive(pz.at[xx], (b_s.at[0], b_r.at[0]), d, to_z)
-        cols, lse = merge([o[z, xx, 32:64, :], pz[xx]], [st[z, xx, 32:64, :], sz[xx]])
+        cols, lse = merge([o[z, xx, 32:64, :], pz[xx]], [st[z, xx, 32:64, :], unpack(sz[xx])])
         if d == 0:
             put(rx.at[x], cols)
-            tx_s[x] = lse
+            tx_s[x] = pack([lse])
         else:
             put(mx.at[d - 1], cols)
-            nx[d - 1] = lse
+            nx[d - 1] = pack([lse])
             outs.append(send(nx.at[d - 1], tx_s.at[x], (d_s.at[1], d_r.at[1]), d, to_x(d)))
             outs.append(send(mx.at[d - 1], rx.at[x], (d_s.at[0], d_r.at[0]), d, to_x(d)))
     for d in (2, 1, 3):
@@ -413,22 +432,24 @@
         arrive(sx.at[xx], (a_s.at[1], a_r.at[1]), d, to_x(4 - d))
         arrive(px.at[xx], (a_s.at[0], a_r.at[0]), d, to_x(4 - d))
     others = [(x + d) % 4 for d in (1, 2, 3)]
+    both_runs = [(unpack(sx[xx], 0), unpack(sx[xx], 1)) for xx in others]
+    first = z == 0
     cols, lse = merge([o[zp, x, 0:32, :]] + [px[xx, zp] for xx in others],
-                      [st[zp, x, 0:32, :]] + [sx[xx, zp] for xx in others])
+                      [st[zp, x, 0:32, :]] + [jnp.where(first, b, a) for a, b in both_runs])
     put(mz, cols)
-    nz[...] = lse
+    nz[...] = pack([lse])
     outs.append(send(nz, tz, (c_s, c_r), 1, to_z))
     outs.append(send(mz, rz, (c_s, c_r), 0, to_z))
     weights[0].wait()
     far = pl.ds(WMID, 2048 - WMID)
     outs.append(send(w_s.at[z, far], w_s.at[z, far], (c_s, c_r), 2, to_z))
     own_cols, own_lse = merge([o[z, x, 0:32, :]] + [px[xx, z] for xx in others],
-                              [st[z, x, 0:32, :]] + [sx[xx, z] for xx in others])
+                              [st[z, x, 0:32, :]] + [jnp.where(first, a, b) for a, b in both_runs])
     mine = x * 4 + y
     put(attg.at[mine, lo], own_cols)
     arrive(tz, (c_s, c_r), 1, to_z)
     arrive(rz, (c_s, c_r), 0, to_z)
-    cols, _ = merge([attg[mine, 0:32, :], rz[...]], [own_lse, tz[...]])
+    cols, _ = merge([attg[mine, 0:32, :], rz[...]], [own_lse, unpack(tz[...])])
     put(attg.at[mine, lo], cols)
 
     slot = lambda x, y: x * 4 + y
@@ -469,7 +490,7 @@
         xx = (x + 4 - d) % 4
         arrive(tx_s.at[xx], (d_s.at[1], d_r.at[1]), d, to_x(4 - d))
         arrive(rx.at[xx], (d_s.at[0], d_r.at[0]), d, to_x(4 - d))
-    cols, _ = merge([rx[i] for i in range(4)], [tx_s[i] for i in range(4)])
+    cols, _ = merge([rx[i] for i in range(4)], [unpack(tx_s[i]) for i in range(4)])
     put(attg.at[mine, hi], cols)
     both(1, 0, 0, 0)
     both(1, 1, 0, 4)
@@ -600,17 +621,18 @@
         out_shape=jax.ShapeDtypeStruct((512, 512), bf),
         scratch_shapes=[
             pltpu.VMEM((2, 4, ROWS, wide), bf), pltpu.VMEM((2, 4, ROWS, 128), f32),
-            pltpu.VMEM((4, 2, 32, wide), bf), pltpu.VMEM((4, 2, 32, 128), f32),
-            pltpu.VMEM((4, 32, wide), bf), pltpu.VMEM((4, 32, 128), f32),
-            pltpu.VMEM((32, wide), bf), pltpu.VMEM((32, 128), f32),
-            pltpu.VMEM((32, wide), bf), pltpu.VMEM((32, 128), f32),
-            pltpu.VMEM((3, 32, wide), bf), pltpu.VMEM((3, 32, 128), f32),
-            pltpu.VMEM((4, 32, wide), bf), pltpu.VMEM((4, 32, 128), f32),
+            pltpu.VMEM((4, 2, 32, wide), bf), pltpu.VMEM((4, 8, 128), f32),
+            pltpu.VMEM((4, 32, wide), bf), pltpu.VMEM((4, 8, 128), f32),
+            pltpu.VMEM((32, wide), bf), pltpu.VMEM((8, 128), f32),
+            pltpu.VMEM((32, wide), bf), pltpu.VMEM((8, 128), f32),
+            pltpu.VMEM((3, 32, wide), bf), pltpu.VMEM((3, 8, 128), f32),
+            pltpu.VMEM((4, 32, wide), bf), pltpu.VMEM((4, 8, 128), f32),
             pltpu.VMEM((16, ROWS, wide), bf), pltpu.VMEM((2, 2048, 512), bf),
             pltpu.VMEM((5, 2, 128, 512), bf), pltpu.VMEM((5, 2, 128, 512), bf), pltpu.VMEM((5, 2, 128, 512), f32),
             pltpu.VMEM((5, 2, 128, 512), bf), pltpu.VMEM((2, 5, 128, 512), bf),
             dma((2, 4)), dma((2, 4)), dma((2, 4)), dma((2, 4)), dma((3,)), dma((3,)), dma((2, 4)), dma((2, 4)),
             dma((2, 20)), dma((2, 20)), dma((5,)), dma((5,)), dma((10,)), dma((2, 10)), dma((5,)),
+            pltpu.VMEM((2, 4, 8, 128), f32),
         ],
         compiler_params=pltpu.CompilerParams(collective_id=1, has_side_effects=True, vmem_limit_bytes=53 << 20),
         name="project",

time: 173 us -> 180 us (1.040)
  Pallas kernels: 170 us -> 177 us
    pallas_call x1, Pallas kernels: 77.3 us -> 83.4 us  [project(): pl.pallas_call(project_kernel, in_specs=[hbm] * 5, out_specs=vmem, out_sh...]
  transfers between devices with their start and end apart: 1 -> 1, of which waited for: 0 -> 0; matrix products, arithmetic and copies ran while one was open for 0% -> 0% of each run, Pallas kernels for 39% -> 38%
where the time goes in v5:
time: 180 us
  Pallas kernels  177 us (98%)
    pallas_call x1, Pallas kernels, project(): pl.pallas_call(project_kernel, in_specs=[hbm] * 5, out_specs=vmem, out_sh...  83.4 us
    pallas_call x1, Pallas kernels, attention(): pl.pallas_call(functools.partial(attn_kernel, nb=nb), in_specs=[smem] * 4...  68.3 us
    pallas_call x1, Pallas kernels, gather(): pl.pallas_call(gather_kernel, in_specs=[hbm] * 6, out_specs=[hbm] * 4, ou...  25.6 us
  transfers between devices with their start and end apart: 1, of which 0 were waited for; matrix products, arithmetic and copies ran while one was open for 0% of the time, Pallas kernels for 38%

profile of v5, /device:TPU:1, one launch (start us, length us, event | category | flops | bytes accessed | tf_op | source)
XLA Modules:
  0.0 179.8 jit_solution(16045941484562468807)
XLA Ops:
  0.0 25.6 %gather.1 = (bf16[8,64,2048]{2,1,0:T(8,128)(2,1)}, bf16[4,2176,128]{2,1,0:T(8,128)(2,1)}, bf16[512,512]{1,0:T(8,128)(2,1)}, bf16[1088,512]{1,0:T(8,128)(2,1)}) custom-call(bf16[64,2048]{1,0:T(8,128)(2,1)} %q.1, bf16[1024,128]{1,0:T(8,128)(2,1)} %ck.1, bf16[1024,128]{1,0:T(8,128)(2,1)} %cv.1, bf16[64,128]{1,0:T(8,128)(2,1)} %nk.1, bf16[64,128]{1,0:T(8,128)(2,1)} %nv.1, ...), custom_call_target="tpu_custom_call" | custom-call | tf_op jit(solution)/shard_map/gather/pallas_call | solution.py:326
  25.6 1.7 collective-permute-start
  27.3 68.3 %attention.1 = (bf16[8,64,2048]{2,1,0:T(8,128)(2,1)}, f32[24,64,128]{2,1,0:T(8,128)}) custom-call(s32[256]{0:T(256)} %cdocs.1, s32[16]{0:T(128)} %ndocs.1, s32[32]{0:T(128)} %tiles.1, s32[1]{0:T(128)} %bitcast.place, bf16[8,64,2048]{2,1,0:T(8,128)(2,1)} %get-tuple-element.11.q_hbm, bf16[8704,128]{1,0:T(8,128)(2,1)} %bitcast.4), custom_call_target="tpu_custom_call" | custom-call | tf_op jit(solution)/shard_map/attention/pallas_call | solution.py:186
  95.6 0.0 collective-permute-done.whi
  95.6 83.4 %project.1 = bf16[512,512]{1,0:T(8,128)(2,1)S(1)} custom-call(bf16[2,4,64,2048]{3,2,1,0:T(8,128)(2,1)} %bitcast.5, f32[6,4,64,128]{3,2,1,0:T(8,128)} %bitcast.6, bf16[2048,512]{1,0:T(8,128)(2,1)} %w.3, bf16[512,512]{1,0:T(8,128)(2,1)} %get-tuple-element.15.wlo, bf16[1088,512]{1,0:T(8,128)(2,1)} %collective-permute-done.whi), custom_call_target="tpu_custom_call" | custom-call | tf_op jit(solution)/shard_map/project/pallas_call | solution.py:617
  179.0 0.8 copy.11
Async XLA Ops:
  25.6 70.0 %collective-permute-start = (bf16[1088,512]{1,0:T(8,128)(2,1)}, bf16[1088,512]{1,0:T(8,128)(2,1)}, u32[]{:S(2)}, u32[]{:S(2)}) collective-permute-start(bf16[1088,512]{1,0:T(8,128)(2,1)} %get-tuple-element.16), channel_id=1, source_target_pairs={{0,64},{4,68},{8,72},{12,76},{16,80},{20,84},{24,88},{28,92},{32,9... | collective-permute-start | bytes 3342344 | tf_op jit(solution)/shard_map/ppermute | solution.py:644
